TPU v7x, 128 devices: a whole 4x4x4 slice. The times are simulated.
128 devices in a mesh: dp: 2 (over x_lo), fsdp: 64 (over x_hi, z, y, core).
Axes of the slice: x: 4 (x_hi: 2, x_lo: 2; x = x_hi * 2 + x_lo), y: 4, z: 4, core: 2. Of those that a mesh axis runs over, the one named last changes fastest.
Arguments:
- states: bfloat16 [32768, 1536], P(('dp', 'fsdp')), may hold values from -24 to 24
- policy: bfloat16 [1536, 256], P('fsdp'), may hold values from -0.15625 to 0.15625
- action_embed: bfloat16 [256, 1536], P('fsdp'), may hold values from -0.375 to 0.375
- norm_gain: bfloat16 [1536], P('fsdp'), may hold values from 0.5 to 1.5
- hidden_in: bfloat16 [1536, 3072], P('fsdp'), may hold values from -0.15625 to 0.15625
- hidden_out: bfloat16 [3072, 1536], P('fsdp'), may hold values from -0.109375 to 0.109375
- precision: float32 [256], replicated, may hold values from 0.25 to 4
- gradient: float32 [1536, 256], P('fsdp'), may hold values from -6 to 6
Outputs:
- update: float32 [1536, 256], P('fsdp')
- residual: float32 [1536, 256], P('fsdp')
All inputs are finite; a program needn't handle non-finite values.
Results may differ from a plain program's by a relative error of at most 0.01.
Values may be sent and summed in bfloat16 or wider, within the bound.
A program may use at most 128 MiB of HBM per device.

v0:
```python
import jax
import jax.numpy as jnp
from jax import lax
from jax.sharding import PartitionSpec as P

ITERS = 2


EPS = 1e-05
DAMPING = 0.1


def contract_last(left, right):
    return lax.dot_general(
        left, right, (((1,), (1,)), ((), ())), preferred_element_type=jnp.float32
    )


def contract_first(left, right):
    return lax.dot_general(
        left, right, (((0,), (0,)), ((), ())), preferred_element_type=jnp.float32
    )


def swish_slope(pre):
    sigma = jax.nn.sigmoid(pre)
    return sigma * (1.0 + pre * (1.0 - sigma))


def norm_back(unit, scale, value):
    return scale * (value - unit * jnp.mean(unit * value, axis=-1, keepdims=True))


def imagine(start, policy, embed, gain, inner, outer):
    first = jnp.tanh(jnp.dot(start, policy, preferred_element_type=jnp.float32))
    mixed = start.astype(jnp.float32) + jnp.dot(
        first.astype(jnp.bfloat16), embed, preferred_element_type=jnp.float32
    )
    scale = lax.rsqrt(jnp.mean(mixed * mixed, axis=-1, keepdims=True) + EPS)
    unit = mixed * scale
    normed = (unit * gain.astype(jnp.float32)).astype(jnp.bfloat16)
    pre = jnp.dot(normed, inner, preferred_element_type=jnp.float32)
    active = jax.nn.silu(pre).astype(jnp.bfloat16)
    later = (mixed + jnp.dot(active, outer, preferred_element_type=jnp.float32)).astype(
        jnp.bfloat16
    )
    second = jnp.tanh(jnp.dot(later, policy, preferred_element_type=jnp.float32))
    return (first, second, later, unit, scale, swish_slope(pre))


def sweeps(
    start,
    first,
    second,
    later,
    unit,
    scale,
    slope,
    direction_b,
    policy,
    embed,
    gain,
    inner,
    outer,
    weighting,
):
    gain_wide = gain.astype(jnp.float32)
    tangent_first = (1.0 - first * first) * jnp.dot(
        start, direction_b, preferred_element_type=jnp.float32
    )
    tangent_mix = jnp.dot(
        tangent_first.astype(jnp.bfloat16), embed, preferred_element_type=jnp.float32
    )
    tangent_norm = (norm_back(unit, scale, tangent_mix) * gain_wide).astype(jnp.bfloat16)
    tangent_active = (
        slope * jnp.dot(tangent_norm, inner, preferred_element_type=jnp.float32)
    ).astype(jnp.bfloat16)
    tangent_later = (
        tangent_mix + jnp.dot(tangent_active, outer, preferred_element_type=jnp.float32)
    ).astype(jnp.bfloat16)
    tangent_second = (1.0 - second * second) * (
        jnp.dot(tangent_later, policy, preferred_element_type=jnp.float32)
        + jnp.dot(later, direction_b, preferred_element_type=jnp.float32)
    )
    cot_second = ((1.0 - second * second) * (weighting * tangent_second)).astype(jnp.bfloat16)
    cot_later = contract_last(cot_second, policy)
    cot_pre = (slope * contract_last(cot_later.astype(jnp.bfloat16), outer)).astype(jnp.bfloat16)
    cot_norm = contract_last(cot_pre, inner) * gain_wide
    cot_mix = cot_later + norm_back(unit, scale, cot_norm)
    cot_first = (
        (1.0 - first * first)
        * (weighting * tangent_first + contract_last(cot_mix.astype(jnp.bfloat16), embed))
    ).astype(jnp.bfloat16)
    return (cot_first, cot_second)


def body(states, policy, action_embed, norm_gain, hidden_in, hidden_out, precision, gradient):
    policy_full, embed_full, gain_full = (
        lax.all_gather(policy, "fsdp", axis=0, tiled=True),
        lax.all_gather(action_embed, "fsdp", axis=0, tiled=True),
        lax.all_gather(norm_gain, "fsdp", axis=0, tiled=True),
    )
    inner, outer = (
        lax.all_gather(hidden_in, "fsdp", axis=0, tiled=True),
        lax.all_gather(hidden_out, "fsdp", axis=0, tiled=True),
    )
    first, second, later, unit, scale, slope = imagine(
        states, policy_full, embed_full, gain_full, inner, outer
    )
    total_rows = states.shape[0] * lax.axis_size("dp") * lax.axis_size("fsdp")
    weighting = precision / total_rows
    update = jnp.zeros_like(gradient)
    residual = gradient
    direction = gradient
    norm_now = lax.psum(jnp.sum(gradient * gradient), "fsdp")
    for turn in range(ITERS):
        direction_b = lax.all_gather(direction.astype(jnp.bfloat16), "fsdp", axis=0, tiled=True)
        cot_first, cot_second = sweeps(
            states,
            first,
            second,
            later,
            unit,
            scale,
            slope,
            direction_b,
            policy_full,
            embed_full,
            gain_full,
            inner,
            outer,
            weighting,
        )
        shard = lax.psum_scatter(
            contract_first(states, cot_first) + contract_first(later, cot_second),
            "fsdp",
            scatter_dimension=0,
            tiled=True,
        )
        image = lax.psum(shard, "dp") + DAMPING * direction
        bend = lax.psum(jnp.sum(direction * image), "fsdp")
        alpha = norm_now / bend
        update = update + alpha * direction
        residual = residual - alpha * image
        if turn + 1 < ITERS:
            norm_next = lax.psum(jnp.sum(residual * residual), "fsdp")
            direction = residual + norm_next / norm_now * direction
            norm_now = norm_next
    return (update, residual)


def solution(mesh):
    placed = (
        P(("dp", "fsdp"), None),
        P("fsdp", None),
        P("fsdp", None),
        P("fsdp"),
        P("fsdp", None),
        P("fsdp", None),
        P(),
        P("fsdp", None),
    )
    return jax.shard_map(
        body,
        mesh=mesh,
        in_specs=placed,
        out_specs=(P("fsdp", None), P("fsdp", None)),
        check_vma=False,
    )
```

profile of v0, /device:TPU:0, one launch (start us, length us, event | category | flops | bytes accessed | tf_op | source)
XLA Modules:
  0.0 1455.7 jit_solution(5247923901160545939)
XLA Ops:
  7.2 0.7 all-gather.4.cloned.1.call-update
  8.0 0.7 all-gather.6.cloned.1.call-update
  8.7 1.2 dynamic-slice
  10.6 0.9 dynamic-update-slice
  11.5 172.4 %all-reduce = bf16[1536]{0:T(1024)(128)(2,1)S(1)} all-reduce(bf16[1536]{0:T(1024)(128)(2,1)S(1)} %dynamic-update-slice), channel_id=1, replica_groups=mesh['dp'=2,'fsdp'=64] {'fsdp'}, use_global_device_ids=true, to_apply=%add | all-reduce | flops 1536 | bytes 6144
  183.9 0.7 convert_element_type.80
  184.6 90.7 %all-gather = bf16[64,4,1536]{2,1,0:T(4,128)(2,1)S(1)} all-gather(bf16[1,4,1536]{2,1,0:T(4,128)(2,1)} %bitcast.53), channel_id=1, replica_groups=mesh['dp'=2,'fsdp'=64] {'fsdp'}, dimensions={0}, use_global_device_ids=true | all-gather | bytes 798720 | tf_op jit(solution)/shard_map/all_gather | solution.py:100
  275.5 92.2 %all_gather.21 = bf16[1536,256]{1,0:T(8,128)(2,1)S(1)} all-gather(bf16[24,256]{1,0:T(8,128)(2,1)S(1)} %copy-done.16), channel_id=1, replica_groups=mesh['dp'=2,'fsdp'=64] {'fsdp'}, dimensions={0}, use_global_device_ids=true | all-gather | bytes 798720 | tf_op jit(solution)/shard_map/all_gather | solution.py:99
  367.7 0.9 copy-done.1
  369.4 90.6 %all_gather.22 = bf16[1536,256]{1,0:T(8,128)(2,1)S(1)} all-gather(bf16[24,256]{1,0:T(8,128)(2,1)S(1)} %convert_element_type.80), channel_id=1, replica_groups=mesh['dp'=2,'fsdp'=64] {'fsdp'}, dimensions={0}, use_global_device_ids=true | all-gather | bytes 798720 | tf_op jit(solution)/shard_map/all_gather | solution.py:117
  460.1 0.9 copy-done.6
  461.4 1.6 multiply_reduce_fusion.3
  463.0 8.0 fusion.25
  471.0 7.4 fusion.4
  478.5 1.1 fusion.18
  479.5 0.9 copy-done.10
  480.5 4.3 fusion
  484.8 8.4 fusion.24
  493.2 1.9 fusion.20
  495.2 1.6 fusion.67
  496.8 12.5 multiply_reduce_fusion.2
  509.2 1.2 broadcast_multiply_fusion.2
  510.5 4.3 convolution_bitcast_fusion.1
  514.8 3.3 convolution_add_fusion.1
  518.1 3.1 copy.39
  521.3 139.6 %reduce-scatter.7.cloned.1.call-done = f32[24,256]{1,0:T(8,128)} async-done(((f32[1536,256]{1,0:T(8,128)}), f32[24,256]{1,0:T(8,128)}) %reduce-scatter.7.cloned.1.call-update) | async-done | bytes 24592 | tf_op jit(solution)/shard_map/reduce_scatter | solution.py:134
  660.8 8.0 psum.43
  668.8 0.6 multiply_reduce_fusion.7
  669.5 163.2 %all-reduce.1 = (f32[]{:T(128)}, f32[]{:T(128)}) all-reduce(f32[]{:T(128)} %get-tuple-element.7, f32[]{:T(128)} %get-tuple-element.6), channel_id=1, replica_groups=mesh['dp'=2,'fsdp'=64] {'fsdp'}, use_global_device_ids=true, to_apply=%region_1.2 | all-reduce | flops 2 | bytes 16 | tf_op jit(solution)/shard_map/psum | solution.py:115
  834.6 163.2 %psum.45 = f32[]{:T(128)} all-reduce(f32[]{:T(128)} %multiply_reduce_fusion.6), channel_id=1, replica_groups=mesh['dp'=2,'fsdp'=64] {'fsdp'}, use_global_device_ids=true, to_apply=%region_10.11 | all-reduce | flops 1 | bytes 8 | tf_op jit(solution)/shard_map/psum | solution.py:146
  999.2 90.5 %all_gather.27 = bf16[1536,256]{1,0:T(8,128)(2,1)S(1)} all-gather(bf16[24,256]{1,0:T(8,128)(2,1)S(1)} %fusion.59), channel_id=1, replica_groups=mesh['dp'=2,'fsdp'=64] {'fsdp'}, dimensions={0}, use_global_device_ids=true | all-gather | bytes 798720 | tf_op jit(solution)/shard_map/all_gather | solution.py:117
  1089.7 0.9 copy-done.7
  1091.8 1.2 copy-done.11
  1093.0 0.6 copy-done.20
  1093.6 7.9 fusion.2
  1101.5 8.4 fusion.23
  1109.9 1.9 fusion.19
  1111.9 1.6 fusion.68
  1113.5 12.5 multiply_reduce_fusion
  1125.9 0.7 broadcast_multiply_fusion
  1126.6 4.2 convolution_bitcast_fusion
  1130.8 2.1 convolution_add_fusion
  1132.9 1.6 copy.41
  1134.6 141.0 %reduce-scatter.9.cloned.1.call-done = f32[24,256]{1,0:T(8,128)} async-done(((f32[1536,256]{1,0:T(8,128)}), f32[24,256]{1,0:T(8,128)}) %reduce-scatter.9.cloned.1.call-update) | async-done | bytes 24592 | tf_op jit(solution)/shard_map/reduce_scatter | solution.py:134
  1275.5 8.0 psum.46
  1283.5 0.6 multiply_reduce_fusion.5
  1284.1 163.1 %psum.47 = f32[]{:T(128)} all-reduce(f32[]{:T(128)} %multiply_reduce_fusion.5), channel_id=1, replica_groups=mesh['dp'=2,'fsdp'=64] {'fsdp'}, use_global_device_ids=true, to_apply=%region_16.17 | all-reduce | flops 1 | bytes 8 | tf_op jit(solution)/shard_map/psum | solution.py:141
  1448.6 0.6 multiply_subtract_fusion.3
  (58 shorter events, 3.3 us)
Async XLA Ops:
  7.2 268.3 %copy-start.17 = (f32[256]{0:T(256)S(1)}, f32[256]{0:T(256)}, u32[]{:S(2)}) copy-start(f32[256]{0:T(256)} %param.14) | copy-start | bytes 3076
  7.2 268.4 %copy-start.16 = (bf16[24,256]{1,0:T(8,128)(2,1)S(1)}, bf16[24,256]{1,0:T(8,128)(2,1)}, u32[]{:S(2)}) copy-start(bf16[24,256]{1,0:T(8,128)(2,1)} %param.9) | copy-start | bytes 36868
  7.2 455.8 %all-gather.4.cloned.1.call-start = ((), (), s32[]{:S(2)}) async-start(), calls=%async_computation.2 | async-start | bytes 9584640 | tf_op jit(solution)/shard_map/all_gather | solution.py:104
  7.9 463.1 %all-gather.6.cloned.1.call-start = ((), (), s32[]{:S(2)}) async-start(), calls=%async_computation.3 | async-start | bytes 9584640 | tf_op jit(solution)/shard_map/all_gather | solution.py:105
  8.7 652.2 %reduce-scatter.7.cloned.1.call-start = ((), (), s32[]{:S(2)}) async-start(), calls=%async_computation.4 | async-start | bytes 1597440 | tf_op jit(solution)/shard_map/reduce_scatter | solution.py:134
  184.6 184.0 %copy-start = (bf16[256,1536]{1,0:T(8,128)(2,1)S(1)}, bf16[256,1536]{1,0:T(8,128)(2,1)}, u32[]{:S(2)}) copy-start(bf16[256,1536]{1,0:T(8,128)(2,1)} %param.8) | copy-start | bytes 2359300
  367.7 0.9 copy-start.1
  460.1 0.9 copy-start.6
  461.4 1.6 copy-start.9
  471.0 7.4 copy-start.2
  471.0 8.5 copy-start.18
  471.0 8.5 copy-start.19
  478.4 1.1 copy-start.5
  478.5 2.0 copy-start.10
  493.2 2.0 copy-start.3
  521.2 147.6 %copy-start.14 = (f32[24,256]{1,0:T(8,128)S(1)}, f32[24,256]{1,0:T(8,128)}, u32[]{:S(2)}) copy-start(f32[24,256]{1,0:T(8,128)} %param.15) | copy-start | bytes 73732
  521.2 754.3 %reduce-scatter.9.cloned.1.call-start = ((), (), s32[]{:S(2)}) async-start(), calls=%async_computation.5 | async-start | bytes 1597440 | tf_op jit(solution)/shard_map/reduce_scatter | solution.py:134
  668.8 422.7 %copy-start.12 = (f32[24,256]{1,0:T(8,128)}, f32[24,256]{1,0:T(8,128)S(1)}, u32[]{:S(2)}) copy-start(f32[24,256]{1,0:T(8,128)S(1)} %psum.43) | copy-start | bytes 73732
  1089.7 0.9 copy-start.7
  1091.0 0.7 copy-start.8
  1091.0 2.6 copy-start.20
  1091.8 1.2 copy-start.11
  1109.9 2.0 copy-start.4
  1134.5 149.0 %copy-start.13 = (f32[24,256]{1,0:T(8,128)S(1)}, f32[24,256]{1,0:T(8,128)}, u32[]{:S(2)}) copy-start(f32[24,256]{1,0:T(8,128)} %copy-done.12) | copy-start | bytes 73732
  1134.5 149.0 %copy-start.15 = (f32[24,256]{1,0:T(8,128)S(1)}, f32[24,256]{1,0:T(8,128)}, u32[]{:S(2)}) copy-start(f32[24,256]{1,0:T(8,128)} %param.15) | copy-start | bytes 73732
Sparse Core Ops, SparseCore 0:
  11.2 87.0 all-gather.3
  101.5 82.9 all-gather.5
  521.3 139.4 reduce-scatter.6
  1134.7 140.8 reduce-scatter.8
where the time goes:
time: 1460 us
  blocking collectives  1040 us (71%)
  waiting for transfers between devices  282 us (19%)
  matrix products  95 us (7%)
  between operations  18.7 us (1%)
    reduce_scatter x2, waiting for transfers between devices, body(): lax.psum_scatter(contract_first(states, cot_first) + contract_first(later...  281 us
    all_gather x2, blocking collectives, body(): lax.all_gather(direction.astype(jnp.bfloat16), 'fsdp', axis=0, tiled=True)  181 us
    unnamed x1, blocking collectives  172 us
    psum x1, blocking collectives, body(): norm_now = lax.psum(jnp.sum(gradient * gradient), 'fsdp')  163 us
    psum x1, blocking collectives, body(): norm_next = lax.psum(jnp.sum(residual * residual), 'fsdp')  163 us
    psum x1, blocking collectives, body(): bend = lax.psum(jnp.sum(direction * image), 'fsdp')  163 us
    all_gather x1, blocking collectives, body(): lax.all_gather(policy, 'fsdp', axis=0, tiled=True)  92.2 us
    all_gather x1, blocking collectives, body(): lax.all_gather(action_embed, 'fsdp', axis=0, tiled=True)  90.7 us
  transfers between devices with their start and end apart: 4, of which 2 were waited for; matrix products, arithmetic and copies ran while one was open for 1% of the time, Pallas kernels for 0%

commit v1 on v0

v1 whole, which is shorter than its diff:
```python
import functools

import jax
import jax.numpy as jnp
from jax import lax
from jax.experimental import pallas as pl
from jax.experimental.pallas import tpu as pltpu
from jax.sharding import PartitionSpec as P

MESH = pl.DeviceIdType.MESH
F32 = jnp.float32
BF16 = jnp.bfloat16
EPS = 1e-05
DAMPING = 0.1
ALL = slice(None)

ROWS = 256
D = 1536
FF = 3072
ACT = 256
TOTAL_ROWS = 32768
N_ITEM = 5
ITEM_SEMS = 41
OTHER_SEMS = 2 + 1 + 3 * 10 + 2 * (1 + 6 + 6 + 3) + (6 + 6 + 1) + 1


def nn(left, right):
    return jnp.dot(left, right, preferred_element_type=F32)


def nt(left, right):
    return lax.dot_general(left, right, (((1,), (1,)), ((), ())), preferred_element_type=F32)


def swish_slope(pre, sigma):
    return sigma * (1.0 + pre * (1.0 - sigma))


def kernel(
    states,
    pack,
    embed_in,
    inner_in,
    outer_in,
    precision,
    out_update,
    out_residual,
    S,
    HI,
    HO,
    pack_far,
    inner_wide,
    inner_far,
    policy,
    embed,
    gain,
    gain_tall,
    going,
    start_t,
    later_t,
    NT,
    AA,
    slope,
    mixed,
    unit,
    scale,
    tmix,
    first_d,
    second_d,
    tfirst,
    later,
    tlater,
    cot_later,
    cot_b,
    cot_pre,
    cot_first,
    cot_second,
    IP,
    RB,
    ACC,
    R1,
    T2,
    R2,
    T3,
    SC,
    g32,
    res32,
    RG,
    out_near,
    out_far,
    send_sem,
    recv_sem,
):
    lo = lax.axis_index("dp")
    f = lax.axis_index("fsdp")
    c = f % 2
    y = (f // 2) % 4
    z = (f // 8) % 4
    hi = f // 32
    x = hi * 2 + lo

    def dev(dx=None, dy=0, dz=0, core=None):
        xx = x if dx is None else (x + dx) % 4
        yy, zz = (y + dy) % 4, (z + dz) % 4
        cc = c if core is None else core
        return (xx % 2, (((xx // 2) * 4 + zz) * 4 + yy) * 2 + cc)

    def axis_dev(axis, d):
        return dev(**{"d" + axis: d})

    opp = ((3 - x) % 2, ((((3 - x) // 2) * 4 + z) * 4 + y) * 2 + c)
    partner = dev(core=1 - c)

    pending = []
    counter = [N_ITEM * ITEM_SEMS]

    def copy(src, dst, sem, to):
        op = pltpu.make_async_remote_copy(
            src_ref=src,
            dst_ref=dst,
            send_sem=send_sem.at[sem],
            recv_sem=recv_sem.at[sem],
            device_id=to,
            device_id_type=MESH,
        )
        op.start()
        pending.append(op)
        return op

    def fresh(n=1):
        base = counter[0]
        counter[0] += n
        return base

    barrier = pltpu.get_barrier_semaphore()
    peers = [partner] + [axis_dev(a, d) for a in ("x", "y", "z") for d in (1, 2, 3)]
    for peer in peers:
        pl.semaphore_signal(barrier, inc=1, device_id=peer, device_id_type=MESH)
    inner_wide[...] = inner_in[...].astype(F32)
    pl.semaphore_wait(barrier, len(peers))

    half = pl.ds(pl.multiple_of((1 - c) * 1536, 128), 1536)
    op_inner = copy(inner_wide.at[:, half], inner_far, fresh(), partner)
    half = pl.ds(pl.multiple_of((1 - c) * 384, 128), 384)
    op_pack = copy(pack.at[:, half], pack_far, fresh(), partner)

    def part(item, t, h, zz, yy, cut):
        if item == 0:
            rows = pl.ds(pl.multiple_of(lo * 32, 32), 32) if cut == 0 else ALL
            if cut == 1:
                rows = pl.ds(pl.multiple_of((1 - lo) * 32, 32), 32)
            return S.at[c, t, h, zz, yy, rows, :]
        cols = ALL
        if cut == 0:
            cols = pl.ds(pl.multiple_of(lo * 128, 128), 128)
        if cut == 1:
            cols = pl.ds(pl.multiple_of((1 - lo) * 128, 128), 128)
        if item < 3:
            return HI.at[c, (item - 1) * 3 + t, h, zz, yy, :, cols]
        return HO.at[(item - 3) * 3 + t, h, zz, yy, c, :, cols]

    one = lambda i: pl.ds(i, 1)
    ops = {}

    def send(item, key, sem, t, h, zz, yy, cut, to):
        ref = part(item, t, h, zz, yy, cut)
        ops[(item, key)] = copy(ref, ref, item * ITEM_SEMS + sem, to)

    def wait(item, *keys):
        for key in keys:
            ops[(item, key)].wait_recv()

    def stage_a(k):
        send(k, "0x", 0, 0, one(hi), one(z), one(y), None, opp)
        for d in (1, 2, 3):
            send(k, "1y%d" % d, 8 + d, 1, one(hi), one(z), one(y), 0, axis_dev("y", d))
            send(k, "2z%d" % d, 18 + d, 2, one(hi), one(z), one(y), None, axis_dev("z", d))

    def stage_b(k):
        wait(k, "0x")
        for d in (1, 2, 3):
            send(k, "0y%d" % d, d, 0, ALL, one(z), one(y), None, axis_dev("y", d))
        wait(k, "1y1", "1y2", "1y3")
        for d in (1, 2, 3):
            send(k, "1z%d" % d, 11 + d, 1, one(hi), one(z), ALL, 0, axis_dev("z", d))
        wait(k, "2z1", "2z2", "2z3")
        send(k, "2x", 22, 2, one(hi), ALL, one(y), None, opp)

    def hand(k, key, sem, t, h, zz, yy, cut):
        send(k, key, 26 + sem, t, h, zz, yy, cut, partner)

    low, high = pl.ds(0, 2), pl.ds(2, 2)
    h0, h1 = pl.ds(0, 1), pl.ds(1, 1)
    zb, zf, zo = (z + 3) % 4, (z + 1) % 4, (z + 2) % 4
    yb, yf, yo = (y + 3) % 4, (y + 1) % 4, (y + 2) % 4

    def x_part(k, d):
        xx = (x + d) % 4
        h = one(xx // 2)
        other = xx % 2
        if k == 0:
            return h, pl.ds(pl.multiple_of(other * 32, 32), 32), ALL
        return h, ALL, pl.ds(pl.multiple_of(other * 128, 128), 128)

    def x_ref(k, d, zz):
        h, rows, cols = x_part(k, d)
        if k == 0:
            return S.at[c, 1, h, zz, :, rows, :]
        if k < 3:
            return HI.at[c, (k - 1) * 3 + 1, h, zz, :, :, cols]
        return HO.at[(k - 3) * 3 + 1, h, zz, :, c, :, cols]

    def x_send(k, key, sem, d, zz, to):
        ref = x_ref(k, d, zz)
        ops[(k, key)] = copy(ref, ref, k * ITEM_SEMS + sem, to)

    def stage_c(k):
        wait(k, "0y1", "0y2", "0y3")
        send(k, "0f", 4, 0, ALL, one(z), ALL, None, axis_dev("z", 1))
        send(k, "0b", 5, 0, ALL, one(z), ALL, None, axis_dev("z", 3))
        wait(k, "1z1", "1z2", "1z3")
        x_send(k, "1f", 15, 0, ALL, axis_dev("x", 1))
        x_send(k, "1b", 16, 0, ALL, axis_dev("x", 3))
        wait(k, "2x")
        send(k, "2f", 23, 2, ALL, ALL, one(y), None, axis_dev("y", 1))
        send(k, "2b", 24, 2, ALL, ALL, one(y), None, axis_dev("y", 3))
        hand(k, "0p0", 0, 0, ALL, one(z), ALL, None)
        x_send(k, "1p0", 26 + 5, 0, ALL, partner)
        hand(k, "2p0", 10, 2, ALL, ALL, one(y), None)

    def stage_d(k):
        wait(k, "0f")
        send(k, "0ff", 6, 0, h0, one(zb), ALL, None, axis_dev("z", 1))
        wait(k, "0b")
        send(k, "0bb", 7, 0, h1, one(zf), ALL, None, axis_dev("z", 3))
        wait(k, "1f")
        x_send(k, "1ff", 17, 3, low, axis_dev("x", 1))
        wait(k, "1b")
        x_send(k, "1bb", 18, 1, high, axis_dev("x", 3))
        wait(k, "2f")
        send(k, "2ff", 25, 2, h0, ALL, one(yb), None, axis_dev("y", 1))
        wait(k, "2b")
        send(k, "2bb", 8, 2, h1, ALL, one(yf), None, axis_dev("y", 3))
        hand(k, "0p1", 1, 0, ALL, one(zb), ALL, None)
        hand(k, "0p2", 2, 0, ALL, one(zf), ALL, None)
        x_send(k, "1p1", 26 + 6, 3, ALL, partner)
        x_send(k, "1p2", 26 + 7, 1, ALL, partner)
        hand(k, "2p1", 11, 2, ALL, ALL, one(yb), None)
        hand(k, "2p2", 12, 2, ALL, ALL, one(yf), None)

    def stage_e(k):
        wait(k, "0ff")
        hand(k, "0p3", 3, 0, h0, one(zo), ALL, None)
        wait(k, "0bb")
        hand(k, "0p4", 4, 0, h1, one(zo), ALL, None)
        wait(k, "1ff")
        x_send(k, "1p3", 26 + 8, 2, low, partner)
        wait(k, "1bb")
        x_send(k, "1p4", 26 + 9, 2, high, partner)
        wait(k, "2ff")
        hand(k, "2p3", 13, 2, h0, ALL, one(yo), None)
        wait(k, "2bb")
        hand(k, "2p4", 14, 2, h1, ALL, one(yo), None)

    def stage_f(k):
        wait(k, *["%dp%d" % (t, i) for t in range(3) for i in range(5)])

    scalar_ops = {}
    scalar_base = fresh(30)
    places = (("core", c, 2), ("y", y, 4), ("z", z, 4), ("x", x, 4))

    def total_send(which, phase, value):
        axis, own, n = places[phase]
        SC[which, phase, own] = value
        ref = SC.at[which, phase, own]
        base = scalar_base + 10 * which + (0, 1, 4, 7)[phase]
        todo = []
        for d in range(1, n):
            to = partner if axis == "core" else axis_dev(axis, d)
            todo.append(copy(ref, ref, base + d - 1, to))
        scalar_ops[(which, phase)] = todo

    def total_take(which, phase):
        for op in scalar_ops[(which, phase)]:
            op.wait_recv()
        n = places[phase][2]
        value = SC[which, phase, 0]
        for i in range(1, n):
            value = value + SC[which, phase, i]
        return value

    def total_step(which, phase):
        value = total_take(which, phase)
        if phase < 3:
            total_send(which, phase + 1, value)
        return value

    def fold(value):
        value = value.reshape(-1, 8, value.shape[-1]).sum(axis=0)
        tile = value[:, 0:128]
        for i in range(1, value.shape[-1] // 128):
            tile = tile + value[:, 128 * i : 128 * i + 128]
        return tile

    def whole(tile):
        return jnp.sum(jnp.sum(tile, axis=1, keepdims=True), axis=0, keepdims=True)

    weigh_rows = outer_in
    for ct in range(6):
        if ct % 3 == 1:
            left = weigh_rows[:, 256 * ct : 256 * ct + 128]
            right = weigh_rows[:, 256 * ct + 128 : 256 * ct + 256]
            HO[ct, hi, z, y, c, :, pl.ds(pl.multiple_of(lo * 128, 128), 128)] = jnp.where(lo == 0, left, right)
        else:
            HO[ct, hi, z, y, c] = weigh_rows[:, 256 * ct : 256 * ct + 256]

    near = pack[:, pl.ds(pl.multiple_of(c * 384, 128), 384)]
    g_own = jnp.concatenate([pack[:, 128:256], pack[:, 512:640]], axis=1)
    total_send(0, 0, fold(g_own * g_own))
    op_pack.wait_recv()
    far = pack_far[...]
    pair = jnp.concatenate([jnp.where(c == 0, near, far), jnp.where(c == 0, far, near)], axis=0)
    g32[hi] = pair[:, 128:256]
    gains = pair[:, 256:384].astype(BF16)
    S[c, 0, hi, z, y, 0:48] = pair[:, 0:128].astype(BF16)
    S[c, 0, hi, z, y, 48:64] = gains[0:16]
    gb = pair[:, 128:256]
    both = jnp.concatenate([gb, pair[16:32, 256:384]], axis=0)
    S[c, 1, hi, z, y, pl.ds(pl.multiple_of(lo * 32, 32), 32)] = jnp.where(lo == 0, both[0:32], both[32:64]).astype(BF16)
    S[c, 2, hi, z, y, 0:48] = embed_in[...]
    S[c, 2, hi, z, y, 48:64] = gains[32:48]
    stage_a(0)
    op_g32 = copy(g32.at[one(hi)], g32.at[one(hi)], fresh(), opp)

    op_inner.wait_recv()
    near = inner_wide[:, pl.ds(pl.multiple_of(c * 1536, 128), 1536)]
    far = inner_far[...]
    pair = jnp.concatenate([jnp.where(c == 0, near, far), jnp.where(c == 0, far, near)], axis=0)
    for ct in range(6):
        if ct % 3 == 1:
            left = pair[:, 256 * ct : 256 * ct + 128]
            right = pair[:, 256 * ct + 128 : 256 * ct + 256]
            HI[c, ct, hi, z, y, :, pl.ds(pl.multiple_of(lo * 128, 128), 128)] = jnp.where(lo == 0, left, right).astype(BF16)
        else:
            HI[c, ct, hi, z, y] = pair[:, 256 * ct : 256 * ct + 256].astype(BF16)
    stage_a(1)
    stage_b(0)
    stage_a(2)
    stage_b(1)
    stage_c(0)
    total_step(0, 0)
    stage_a(3)
    stage_a(4)
    stage_c(1)
    stage_b(2)
    stage_d(0)
    total_step(0, 1)

    @pl.loop(0, 6)
    def _(i):
        s = pl.ds(pl.multiple_of(i * 256, 256), 256)
        start_t[s, :] = states[:, s].astype(F32).T.astype(BF16)

    stage_e(0)
    total_step(0, 2)
    stage_c(2)
    stage_f(0)
    rr = whole(total_step(0, 3)) * 0.5

    for t in range(3):
        for a in range(2):
            for b in range(4):
                gain_tall[a, b, :, 16 * t : 16 * t + 16] = S[0, t, a, b, :, 48:64]
    pick = (lax.broadcasted_iota(jnp.int32, (16, 128), 1) == 0).astype(BF16)
    gain[...] = nt(pick, gain_tall[...].reshape(D, 128))[0:8]
    for cc in range(2):
        for a in range(2):
            policy[768 * a : 768 * a + 768, 128 * cc : 128 * cc + 128] = S[cc, 0, a, :, :, 0:48].reshape(768, 128)
            going[768 * a : 768 * a + 768, 128 * cc : 128 * cc + 128] = S[cc, 1, a, :, :, 0:48].reshape(768, 128)
    for q in range(4):
        total = jnp.zeros((ACT, 384), F32)
        for cc in range(2):
            out_row = lax.broadcasted_iota(jnp.int32, (ACT, 512), 0)
            in_row = lax.broadcasted_iota(jnp.int32, (ACT, 512), 1)
            want = (lax.div(out_row, 8) * 16) + 4 * q + lax.rem(out_row, 4)
            mine = lax.rem(lax.div(out_row, 4), 2) == cc
            choose = jnp.where(mine & (in_row == want), 1.0, 0.0).astype(BF16)
            block = jnp.concatenate(
                [S[cc, 2, :, :, :, 16 * s : 16 * s + 16].reshape(512, 128) for s in range(3)], axis=1
            )
            total = total + nn(choose, block)
        embed[:, 384 * q : 384 * q + 384] = total.astype(BF16)

    def blocks(n):
        return pl.loop(0, ROWS // n)

    first = jnp.tanh(nn(states[...], policy[...]))
    first_d[...] = 1.0 - first * first
    mixed[...] = nn(first.astype(BF16), embed[...])
    tfirst[...] = first_d[...] * nn(states[...], going[...])
    tmix[...] = nn(tfirst[...].astype(BF16), embed[...])

    @blocks(32)
    def _(i):
        s = pl.ds(pl.multiple_of(i * 32, 32), 32)
        m = states[s, :].astype(F32) + mixed[s, :]
        mixed[s, :] = m
        r = lax.rsqrt(jnp.mean(m * m, axis=-1, keepdims=True) + EPS)
        scale[s, :] = jnp.broadcast_to(r, (32, 128))
        u = m * r
        unit[s, :] = u
        g = gain[0:1, :]
        NT[s, :] = (u * g).astype(BF16)

    def tangent_norm(offset):
        @blocks(32)
        def _(i):
            s = pl.ds(pl.multiple_of(i * 32, 32), 32)
            o = pl.ds(pl.multiple_of(i * 32 + offset, 32), 32)
            u, v, g = unit[s, :], tmix[s, :], gain[0:1, :]
            w = scale[s, 0:1] * (v - u * jnp.mean(u * v, axis=-1, keepdims=True))
            NT[o, :] = (w * g).astype(BF16)

    tangent_norm(256)

    stage_d(1)
    stage_b(3)
    stage_e(1)
    stage_d(2)
    stage_c(3)
    stage_b(4)
    stage_f(1)

    def take_inner(ch):
        for cc in range(2):
            @pl.loop(0, 3)
            def _(t):
                w = HI[cc, ch * 3 + t].reshape(D, 256)
                cols = pl.ds(pl.multiple_of(cc * 1536 + ch * 768 + t * 256, 256), 256)
                pre = nn(NT[0:256, :], w)
                sigma = jax.nn.sigmoid(pre)
                AA[0:256, cols] = (pre * sigma).astype(BF16)
                sl = swish_slope(pre, sigma)
                slope[:, cols] = sl
                AA[256:512, cols] = (sl * nn(NT[256:512, :], w)).astype(BF16)

    take_inner(0)
    stage_e(2)
    stage_d(3)
    stage_c(4)
    stage_f(2)
    take_inner(1)
    stage_e(3)
    stage_d(4)
    stage_f(3)

    def take_outer(ch):
        @pl.loop(0, 3)
        def _(t):
            w = HO[ch * 3 + t].reshape(FF, 256)
            cols = pl.ds(pl.multiple_of(ch * 768 + t * 256, 256), 256)
            l = (mixed[:, cols] + nn(AA[0:256, :], w)).astype(BF16)
            later[:, cols] = l
            later_t[cols, :] = l.astype(F32).T.astype(BF16)
            tlater[:, cols] = (tmix[:, cols] + nn(AA[256:512, :], w)).astype(BF16)

    take_outer(0)
    stage_e(4)
    stage_f(4)
    take_outer(1)
    op_g32.wait_recv()

    second = jnp.tanh(nn(later[...], policy[...]))
    second_d[...] = 1.0 - second * second
    weighting = precision[...] * (1.0 / TOTAL_ROWS)

    def finish_sweep(it):
        tsecond = second_d[...] * (nn(tlater[...], policy[...]) + nn(later[...], going[...]))
        tf = tfirst[...]
        total_send(1 + it, 0, fold(weighting * (tf * tf + tsecond * tsecond)))
        cs = (second_d[...] * (weighting * tsecond)).astype(BF16)
        cot_second[...] = cs
        cl = nt(cs, policy[...])
        cot_later[...] = cl
        cot_b[...] = cl.astype(BF16)

        @pl.loop(0, 4)
        def _(i):
            a, b = i // 2, i % 2
            acc = jnp.zeros((ROWS, 768), F32)
            for ct in range(6):
                w = HO[ct, a, pl.ds(b * 2, 2)].reshape(768, 256)
                acc = acc + nt(cot_b[:, 256 * ct : 256 * ct + 256], w)
            cols = pl.ds(pl.multiple_of(i * 768, 256), 768)
            cot_pre[:, cols] = (slope[:, cols] * acc).astype(BF16)

        total_step(1 + it, 0)

        @pl.loop(0, 2)
        def _(a):
            acc = jnp.zeros((ROWS, 768), F32)
            for n in range(12):
                w = HI[n // 6, n % 6, a].reshape(768, 256)
                acc = acc + nt(cot_pre[:, 256 * n : 256 * n + 256], w)
            cols = pl.ds(pl.multiple_of(a * 768, 256), 768)
            tmix[:, cols] = acc

        total_step(1 + it, 1)

        @blocks(32)
        def _(i):
            s = pl.ds(pl.multiple_of(i * 32, 32), 32)
            u, g = unit[s, :], gain[0:1, :]
            v = tmix[s, :] * g
            w = scale[s, 0:1] * (v - u * jnp.mean(u * v, axis=-1, keepdims=True))
            cot_b[s, :] = (cot_later[s, :] + w).astype(BF16)

        cf = (first_d[...] * (weighting * tfirst[...] + nt(cot_b[...], embed[...]))).astype(BF16)
        cot_first[...] = cf

    r_base = [fresh(16), fresh(16)]
    gather_base = fresh(13)

    def sum_image(it):
        base = r_base[it]

        @pl.loop(0, 6)
        def _(i):
            s = pl.ds(pl.multiple_of(i * 256, 256), 256)
            v = nn(start_t[s, :], cot_first[...]) + nn(later_t[s, :], cot_second[...])
            IP[it, 0, s, :] = v[:, 0:128]
            IP[it, 1, s, :] = v[:, 128:256]

        op = copy(IP.at[it, 1 - c], RB.at[it], base, partner)
        total_step(1 + it, 2)
        op.wait_recv()
        for a in range(2):
            rows = slice(768 * a, 768 * a + 768)
            ACC[it, a] = (IP[it, c, rows, :] + RB[it, rows, :]).reshape(4, 4, 48, 128)
        todo = []
        for d in (1, 2, 3):
            todo.append(copy(ACC.at[it, 0, :, (y + d) % 4], R1.at[it, 0, d - 1], base + d, axis_dev("y", d)))
            todo.append(copy(ACC.at[it, 1, (z + d) % 4], R1.at[it, 1, d - 1], base + 3 + d, axis_dev("z", d)))
        total = whole(total_step(1 + it, 3))
        for op in todo:
            op.wait_recv()
        T2[it, 0] = ACC[it, 0, :, y] + R1[it, 0, 0] + R1[it, 0, 1] + R1[it, 0, 2]
        T2[it, 1] = ACC[it, 1, z] + R1[it, 1, 0] + R1[it, 1, 1] + R1[it, 1, 2]
        todo = []
        for d in (1, 2, 3):
            todo.append(copy(T2.at[it, 0, (z + d) % 4], R2.at[it, 0, d - 1], base + 6 + d, axis_dev("z", d)))
            todo.append(copy(T2.at[it, 1, (y + d) % 4], R2.at[it, 1, d - 1], base + 9 + d, axis_dev("y", d)))
        for op in todo:
            op.wait_recv()
        T3[it, x, 0] = T2[it, 0, z] + R2[it, 0, 0] + R2[it, 0, 1] + R2[it, 0, 2]
        T3[it, x, 1] = T2[it, 1, y] + R2[it, 1, 0] + R2[it, 1, 1] + R2[it, 1, 2]
        todo = []
        for d in (1, 2, 3):
            todo.append(copy(T3.at[it, x], T3.at[it, x], base + 12 + d, axis_dev("x", d)))
        for op in todo:
            op.wait_recv()
        return total

    finish_sweep(0)
    bend = sum_image(0) + DAMPING * rr
    alpha1 = rr / bend
    image = T3[0, 0] + T3[0, 1] + T3[0, 2] + T3[0, 3]
    residual = g32[...] - alpha1 * (image + DAMPING * g32[...])
    res32[...] = residual
    RG[c, 0, z, y] = residual[0].astype(BF16)
    RG[c, 1, z, y] = residual[1].astype(BF16)
    todo = []
    for d in (1, 2, 3):
        ref = RG.at[c, 0, z, y]
        todo.append(copy(ref, ref, gather_base + d - 1, axis_dev("y", d)))
        ref = RG.at[c, 1, z, y]
        todo.append(copy(ref, ref, gather_base + d + 2, axis_dev("z", d)))
    for op in todo:
        op.wait_recv()
    todo = []
    for d in (1, 2, 3):
        ref = RG.at[c, 0, z]
        todo.append(copy(ref, ref, gather_base + d + 5, axis_dev("z", d)))
        ref = RG.at[c, 1, :, y]
        todo.append(copy(ref, ref, gather_base + d + 8, axis_dev("y", d)))
    for op in todo:
        op.wait_recv()
    op = copy(RG.at[c], RG.at[c], gather_base + 12, partner)
    op.wait_recv()

    tile = jnp.zeros((8, 128), F32)
    for cc in range(2):
        r = RG[cc].astype(F32).reshape(D, 128)
        tile = tile + fold(r * r)
    new = whole(tile)
    beta = new / rr
    tile = jnp.zeros((8, 128), F32)
    for cc in range(2):
        r = RG[cc].astype(F32).reshape(D, 128)
        cols = slice(128 * cc, 128 * cc + 128)
        v = r + beta * going[:, cols].astype(F32)
        tile = tile + fold(v * v)
        going[:, cols] = v.astype(BF16)
    dd = whole(tile)

    tfirst[...] = first_d[...] * nn(states[...], going[...])
    tmix[...] = nn(tfirst[...].astype(BF16), embed[...])
    tangent_norm(256)
    for cc in range(2):
        @pl.loop(0, 6)
        def _(t):
            cols = pl.ds(pl.multiple_of(cc * 1536 + t * 256, 256), 256)
            w = HI[cc, t].reshape(D, 256)
            AA[256:512, cols] = (slope[:, cols] * nn(NT[256:512, :], w)).astype(BF16)

    @pl.loop(0, 6)
    def _(t):
        cols = pl.ds(pl.multiple_of(t * 256, 256), 256)
        w = HO[t].reshape(FF, 256)
        tlater[:, cols] = (tmix[:, cols] + nn(AA[256:512, :], w)).astype(BF16)

    finish_sweep(1)
    bend = sum_image(1) + DAMPING * dd
    alpha2 = new / bend
    image = T3[1, 0, hi] + T3[1, 1, hi] + T3[1, 2, hi] + T3[1, 3, hi]
    g = g32[hi]
    res = res32[hi]
    direction = res + beta * g
    new_update = alpha1 * g + alpha2 * direction
    new_residual = res - alpha2 * (image + DAMPING * direction)
    out_near[0] = jnp.where(c == 0, new_update[24:48], new_update[0:24])
    out_near[1] = jnp.where(c == 0, new_residual[24:48], new_residual[0:24])
    op = copy(out_near, out_far, fresh(), partner)
    mine_u = jnp.where(c == 0, new_update[0:24], new_update[24:48])
    mine_r = jnp.where(c == 0, new_residual[0:24], new_residual[24:48])
    op.wait_recv()
    for mine, k, out in ((mine_u, 0, out_update), (mine_r, 1, out_residual)):
        other = out_far[k]
        out[:, 0:128] = jnp.where(c == 0, mine, other)
        out[:, 128:256] = jnp.where(c == 0, other, mine)
    for op in pending:
        op.wait_send()


def body(states, policy, action_embed, norm_gain, hidden_in, hidden_out, precision, gradient):
    wide = policy.astype(F32)
    gains = jnp.broadcast_to(norm_gain.astype(F32)[:, None], (norm_gain.shape[0], 128))
    pack = jnp.concatenate(
        [wide[:, 0:128], gradient[:, 0:128], gains, wide[:, 128:256], gradient[:, 128:256], gains], axis=1
    )
    embed = action_embed.reshape(4, 4, 3, 128).transpose(2, 1, 0, 3).reshape(48, 128)
    vmem = pl.BlockSpec(memory_space=pltpu.VMEM)
    shapes = [
        ((2, 3, 2, 4, 4, 64, 128), BF16),
        ((2, 6, 2, 4, 4, 48, 256), BF16),
        ((6, 2, 4, 4, 2, 48, 256), BF16),
        ((24, 384), F32),
        ((24, 3072), F32),
        ((24, 1536), F32),
        ((D, ACT), BF16),
        ((ACT, D), BF16),
        ((8, D), F32),
        ((2, 4, 4, 48, 128), BF16),
        ((D, ACT), BF16),
        ((D, ROWS), BF16),
        ((D, ROWS), BF16),
        ((512, D), BF16),
        ((512, FF), BF16),
        ((ROWS, FF), F32),
        ((ROWS, D), F32),
        ((ROWS, D), F32),
        ((ROWS, 128), F32),
        ((ROWS, D), F32),
        ((ROWS, ACT), F32),
        ((ROWS, ACT), F32),
        ((ROWS, ACT), F32),
        ((ROWS, D), BF16),
        ((ROWS, D), BF16),
        ((ROWS, D), F32),
        ((ROWS, D), BF16),
        ((ROWS, FF), BF16),
        ((ROWS, ACT), BF16),
        ((ROWS, ACT), BF16),
        ((2, 2, D, 128), F32),
        ((2, D, 128), F32),
        ((2, 2, 4, 4, 48, 128), F32),
        ((2, 2, 3, 4, 48, 128), F32),
        ((2, 2, 4, 48, 128), F32),
        ((2, 2, 3, 48, 128), F32),
        ((2, 4, 2, 48, 128), F32),
        ((3, 4, 4, 8, 128), F32),
        ((2, 48, 128), F32),
        ((2, 48, 128), F32),
        ((2, 2, 4, 4, 48, 128), BF16),
        ((2, 24, 128), F32),
        ((2, 24, 128), F32),
    ]
    n_sems = N_ITEM * ITEM_SEMS + OTHER_SEMS
    out = jax.ShapeDtypeStruct(gradient.shape, F32)
    return pl.pallas_call(
        kernel,
        out_shape=(out, out),
        in_specs=[vmem] * 6,
        out_specs=(vmem, vmem),
        scratch_shapes=[pltpu.VMEM(s, t) for s, t in shapes]
        + [pltpu.SemaphoreType.DMA((n_sems,)), pltpu.SemaphoreType.DMA((n_sems,))],
        compiler_params=pltpu.CompilerParams(
            collective_id=0, has_side_effects=True, vmem_limit_bytes=62 * 2**20
        ),
        name="natural_step",
    )(states, pack, embed, hidden_in, hidden_out, precision.reshape(1, ACT))


def solution(mesh):
    placed = (
        P(("dp", "fsdp"), None),
        P("fsdp", None),
        P("fsdp", None),
        P("fsdp"),
        P("fsdp", None),
        P("fsdp", None),
        P(),
        P("fsdp", None),
    )
    return jax.shard_map(
        body,
        mesh=mesh,
        in_specs=placed,
        out_specs=(P("fsdp", None), P("fsdp", None)),
        check_vma=False,
    )
```

time: 1460 us -> 160 us (0.11)
  blocking collectives: 1040 us -> 0 us
  waiting for transfers between devices: 282 us -> 0 us
  Pallas kernels: 0 us -> 153 us
  matrix products: 95 us -> 0 us
  between operations: 18.7 us -> 0.67 us
    psum x5 -> x0, blocking collectives: 505 us -> none  [the longest x1 163 us: body(): norm_now = lax.psum(jnp.sum(gradient * gradient), 'fsdp')]
    all_gather x4 -> x0, blocking collectives: 364 us -> none  [the longest x2 181 us: body(): lax.all_gather(direction.astype(jnp.bfloat16), 'fsdp', axis=0, tiled=True)]
    reduce_scatter x2 -> x0, waiting for transfers between devices: 281 us -> none  [body(): lax.psum_scatter(contract_first(states, cot_first) + contract_first(later...]
    unnamed x1 -> x0, blocking collectives: 172 us -> none
    pallas_call x0 -> x1, Pallas kernels: none -> 153 us  [body(): pl.pallas_call(kernel, out_shape=(out, out), in_specs=[vmem] * 6, out_spe...]
    dot_general x23 -> x0, matrix products: 95 us -> none  [the longest x4 28.2 us: contract_last(): lax.dot_general(left, right, (((1,), (1,)), ((), ())), preferred_element_...]
  transfers between devices with their start and end apart: 4 -> 0, of which waited for: 2 -> 0; matrix products, arithmetic and copies ran while one was open for 1% -> 0% of each run, Pallas kernels for 0% -> 0%
where the time goes in v1:
time: 160 us; the launch traced here: 158 us
  Pallas kernels  153 us (96%)
  local copies, waits for them, and re-layouts  4.04 us (3%)
    pallas_call x1, Pallas kernels, body(): pl.pallas_call(kernel, out_shape=(out, out), in_specs=[vmem] * 6, out_spe...  153 us
    unnamed x17, local copies, waits for them, and re-layouts  3.34 us

profile of v1, /device:TPU:0, one launch (start us, length us, event | category | flops | bytes accessed | tf_op | source)
XLA Modules:
  0.0 158.1 jit_solution(9591482811708098821)
XLA Ops:
  0.6 0.0 copy-start.1
  0.6 0.7 convert_element_type.6
  1.4 0.0 copy-done.1
  1.4 0.0 copy-start.4
  1.4 0.6 copy-done.4
  2.0 0.1 constant_dynamic-update-slice_fusion.3
  2.1 0.0 copy-start.3
  2.1 0.1 constant_dynamic-update-slice_fusion.pack
  2.2 0.6 copy-done.3
  2.8 0.0 copy-start
  2.8 0.6 copy.11
  3.5 0.0 copy-done
  3.5 152.7 %natural_step.1 = (f32[24,256]{1,0:T(8,128)}, f32[24,256]{1,0:T(8,128)}) custom-call(bf16[256,1536]{1,0:T(8,128)(2,1)} %states.1, f32[24,768]{1,0:T(8,128)} %copy-done, bf16[48,128]{1,0:T(8,128)(2,1)} %bitcast.4, bf16[24,3072]{1,0:T(8,128)(2,1)} %inner_in.1, bf16[48,1536]{1,0:T(8,128)(2,1)} %outer_in.1, f32[1,256]{1,0:T(1,128)} %bitcast.5), custom_call_target="tpu_custom_call" | custom-call | tf_op jit(solution)/shard_map/natural_step/pallas_call | solution.py:700
  156.1 0.0 copy-start.2
  156.1 1.4 copy.19
  157.5 0.0 copy-done.2
  157.5 0.6 copy.20
  (6 shorter events, 0.0 us)
Async XLA Ops:
  0.6 0.7 copy-start.1
  1.4 0.7 copy-start.4
  2.1 0.7 copy-start.3
  2.8 0.6 copy-start
  156.1 1.4 copy-start.2

commit v2 on v1

--- a/solution.py
+++ b/solution.py
@@ -21,7 +21,7 @@
 TOTAL_ROWS = 32768
 N_ITEM = 5
 ITEM_SEMS = 41
-OTHER_SEMS = 2 + 1 + 3 * 10 + 2 * (1 + 6 + 6 + 3) + (6 + 6 + 1) + 1
+OTHER_SEMS = 2 + 1 + 6 + 30 + 2 * 17 + 20 + 1
 
 
 def nn(left, right):
@@ -38,17 +38,21 @@
 
 def kernel(
     states,
-    pack,
+    policy_in,
     embed_in,
+    gain_in,
     inner_in,
     outer_in,
     precision,
+    gradient,
     out_update,
     out_residual,
     S,
     HI,
     HO,
+    pack,
     pack_far,
+    embed_near,
     inner_wide,
     inner_far,
     policy,
@@ -76,18 +80,21 @@
     cot_first,
     cot_second,
     IP,
+    IPW,
     RB,
     ACC,
+    ACCW,
     R1,
     T2,
+    T2W,
     R2,
     T3,
     SC,
     g32,
     res32,
     RG,
-    out_near,
-    out_far,
+    res_near,
+    res_far,
     send_sem,
     recv_sem,
 ):
@@ -137,6 +144,18 @@
     for peer in peers:
         pl.semaphore_signal(barrier, inc=1, device_id=peer, device_id_type=MESH)
     inner_wide[...] = inner_in[...].astype(F32)
+    diagonal = lax.broadcasted_iota(jnp.int32, (24, 24), 0) == lax.broadcasted_iota(jnp.int32, (24, 24), 1)
+    gain_row = jnp.broadcast_to(gain_in[...].astype(F32), (24, 24))
+    gain_column = jnp.sum(jnp.where(diagonal, gain_row, 0.0), axis=1, keepdims=True)
+    for core in range(2):
+        pack[:, 384 * core : 384 * core + 128] = policy_in[:, 128 * core : 128 * core + 128].astype(F32)
+        pack[:, 384 * core + 128 : 384 * core + 256] = gradient[:, 128 * core : 128 * core + 128]
+        pack[:, 384 * core + 256 : 384 * core + 384] = jnp.broadcast_to(gain_column, (24, 128))
+    wide = embed_in[...].astype(F32)
+    for q in range(4):
+        for s in range(3):
+            column = 384 * q + 128 * s
+            embed_near[16 * s + 4 * q : 16 * s + 4 * q + 4, :] = wide[:, column : column + 128]
     pl.semaphore_wait(barrier, len(peers))
 
     half = pl.ds(pl.multiple_of((1 - c) * 1536, 128), 1536)
@@ -214,21 +233,34 @@
         ref = x_ref(k, d, zz)
         ops[(k, key)] = copy(ref, ref, k * ITEM_SEMS + sem, to)
 
+    fine_base = fresh(6)
+
     def stage_c(k):
+        fine = k == N_ITEM - 1
+        f0, b0, fl, bl = (h0, h1, low, high) if fine else (ALL, ALL, ALL, ALL)
         wait(k, "0y1", "0y2", "0y3")
-        send(k, "0f", 4, 0, ALL, one(z), ALL, None, axis_dev("z", 1))
-        send(k, "0b", 5, 0, ALL, one(z), ALL, None, axis_dev("z", 3))
+        send(k, "0f", 4, 0, f0, one(z), ALL, None, axis_dev("z", 1))
+        send(k, "0b", 5, 0, b0, one(z), ALL, None, axis_dev("z", 3))
         wait(k, "1z1", "1z2", "1z3")
-        x_send(k, "1f", 15, 0, ALL, axis_dev("x", 1))
-        x_send(k, "1b", 16, 0, ALL, axis_dev("x", 3))
+        x_send(k, "1f", 15, 0, fl, axis_dev("x", 1))
+        x_send(k, "1b", 16, 0, bl, axis_dev("x", 3))
         wait(k, "2x")
-        send(k, "2f", 23, 2, ALL, ALL, one(y), None, axis_dev("y", 1))
-        send(k, "2b", 24, 2, ALL, ALL, one(y), None, axis_dev("y", 3))
+        send(k, "2f", 23, 2, f0, ALL, one(y), None, axis_dev("y", 1))
+        send(k, "2b", 24, 2, b0, ALL, one(y), None, axis_dev("y", 3))
+        if fine:
+            sem = fine_base - k * ITEM_SEMS
+            send(k, "0F", sem, 0, h1, one(z), ALL, None, axis_dev("z", 1))
+            send(k, "0B", sem + 1, 0, h0, one(z), ALL, None, axis_dev("z", 3))
+            x_send(k, "1F", sem + 2, 0, high, axis_dev("x", 1))
+            x_send(k, "1B", sem + 3, 0, low, axis_dev("x", 3))
+            send(k, "2F", sem + 4, 2, h1, ALL, one(y), None, axis_dev("y", 1))
+            send(k, "2B", sem + 5, 2, h0, ALL, one(y), None, axis_dev("y", 3))
         hand(k, "0p0", 0, 0, ALL, one(z), ALL, None)
         x_send(k, "1p0", 26 + 5, 0, ALL, partner)
         hand(k, "2p0", 10, 2, ALL, ALL, one(y), None)
 
     def stage_d(k):
+        fine = k == N_ITEM - 1
         wait(k, "0f")
         send(k, "0ff", 6, 0, h0, one(zb), ALL, None, axis_dev("z", 1))
         wait(k, "0b")
@@ -241,10 +273,16 @@
         send(k, "2ff", 25, 2, h0, ALL, one(yb), None, axis_dev("y", 1))
         wait(k, "2b")
         send(k, "2bb", 8, 2, h1, ALL, one(yf), None, axis_dev("y", 3))
+        if fine:
+            wait(k, "0F", "0B")
         hand(k, "0p1", 1, 0, ALL, one(zb), ALL, None)
         hand(k, "0p2", 2, 0, ALL, one(zf), ALL, None)
+        if fine:
+            wait(k, "1F", "1B")
         x_send(k, "1p1", 26 + 6, 3, ALL, partner)
         x_send(k, "1p2", 26 + 7, 1, ALL, partner)
+        if fine:
+            wait(k, "2F", "2B")
         hand(k, "2p1", 11, 2, ALL, ALL, one(yb), None)
         hand(k, "2p2", 12, 2, ALL, ALL, one(yf), None)
 
@@ -314,8 +352,10 @@
         else:
             HO[ct, hi, z, y, c] = weigh_rows[:, 256 * ct : 256 * ct + 256]
 
+    stage_a(3)
+    stage_a(4)
     near = pack[:, pl.ds(pl.multiple_of(c * 384, 128), 384)]
-    g_own = jnp.concatenate([pack[:, 128:256], pack[:, 512:640]], axis=1)
+    g_own = gradient[...]
     total_send(0, 0, fold(g_own * g_own))
     op_pack.wait_recv()
     far = pack_far[...]
@@ -327,7 +367,7 @@
     gb = pair[:, 128:256]
     both = jnp.concatenate([gb, pair[16:32, 256:384]], axis=0)
     S[c, 1, hi, z, y, pl.ds(pl.multiple_of(lo * 32, 32), 32)] = jnp.where(lo == 0, both[0:32], both[32:64]).astype(BF16)
-    S[c, 2, hi, z, y, 0:48] = embed_in[...]
+    S[c, 2, hi, z, y, 0:48] = embed_near[...].astype(BF16)
     S[c, 2, hi, z, y, 48:64] = gains[32:48]
     stage_a(0)
     op_g32 = copy(g32.at[one(hi)], g32.at[one(hi)], fresh(), opp)
@@ -344,26 +384,26 @@
         else:
             HI[c, ct, hi, z, y] = pair[:, 256 * ct : 256 * ct + 256].astype(BF16)
     stage_a(1)
+    stage_a(2)
+    stage_b(3)
     stage_b(0)
-    stage_a(2)
     stage_b(1)
     stage_c(0)
     total_step(0, 0)
-    stage_a(3)
-    stage_a(4)
+    stage_b(2)
     stage_c(1)
-    stage_b(2)
+    stage_b(4)
+    total_step(0, 1)
     stage_d(0)
-    total_step(0, 1)
 
     @pl.loop(0, 6)
     def _(i):
         s = pl.ds(pl.multiple_of(i * 256, 256), 256)
         start_t[s, :] = states[:, s].astype(F32).T.astype(BF16)
 
+    stage_c(2)
     stage_e(0)
     total_step(0, 2)
-    stage_c(2)
     stage_f(0)
     rr = whole(total_step(0, 3)) * 0.5
 
@@ -394,6 +434,9 @@
     def blocks(n):
         return pl.loop(0, ROWS // n)
 
+    stage_d(1)
+    stage_c(3)
+
     first = jnp.tanh(nn(states[...], policy[...]))
     first_d[...] = 1.0 - first * first
     mixed[...] = nn(first.astype(BF16), embed[...])
@@ -423,17 +466,14 @@
 
     tangent_norm(256)
 
-    stage_d(1)
-    stage_b(3)
     stage_e(1)
     stage_d(2)
-    stage_c(3)
-    stage_b(4)
+    stage_c(4)
     stage_f(1)
 
     def take_inner(ch):
         for cc in range(2):
-            @pl.loop(0, 3)
+            @pl.loop(0, 3, unroll=True)
             def _(t):
                 w = HI[cc, ch * 3 + t].reshape(D, 256)
                 cols = pl.ds(pl.multiple_of(cc * 1536 + ch * 768 + t * 256, 256), 256)
@@ -447,7 +487,6 @@
     take_inner(0)
     stage_e(2)
     stage_d(3)
-    stage_c(4)
     stage_f(2)
     take_inner(1)
     stage_e(3)
@@ -455,7 +494,7 @@
     stage_f(3)
 
     def take_outer(ch):
-        @pl.loop(0, 3)
+        @pl.loop(0, 3, unroll=True)
         def _(t):
             w = HO[ch * 3 + t].reshape(FF, 256)
             cols = pl.ds(pl.multiple_of(ch * 768 + t * 256, 256), 256)
@@ -484,7 +523,7 @@
         cot_later[...] = cl
         cot_b[...] = cl.astype(BF16)
 
-        @pl.loop(0, 4)
+        @pl.loop(0, 4, unroll=True)
         def _(i):
             a, b = i // 2, i % 2
             acc = jnp.zeros((ROWS, 768), F32)
@@ -496,7 +535,7 @@
 
         total_step(1 + it, 0)
 
-        @pl.loop(0, 2)
+        @pl.loop(0, 2, unroll=True)
         def _(a):
             acc = jnp.zeros((ROWS, 768), F32)
             for n in range(12):
@@ -518,75 +557,113 @@
         cf = (first_d[...] * (weighting * tfirst[...] + nt(cot_b[...], embed[...]))).astype(BF16)
         cot_first[...] = cf
 
-    r_base = [fresh(16), fresh(16)]
-    gather_base = fresh(13)
+    r_base = [fresh(17), fresh(17)]
+    gather_base = fresh(20)
+
+    def halves(v, it):
+        if it == 0:
+            low_half, high_half = v[:, 0:128], v[:, 128:256]
+            low_half, high_half = low_half.reshape(16, 48, 128), high_half.reshape(16, 48, 128)
+        else:
+            v = v.reshape(16, 48, 256)
+            low_half = jnp.concatenate([v[:, 0:24, 0:128], v[:, 0:24, 128:256]], axis=1)
+            high_half = jnp.concatenate([v[:, 24:48, 0:128], v[:, 24:48, 128:256]], axis=1)
+        return jnp.where(c == 0, low_half, high_half), jnp.where(c == 0, high_half, low_half)
 
     def sum_image(it):
         base = r_base[it]
-
-        @pl.loop(0, 6)
-        def _(i):
-            s = pl.ds(pl.multiple_of(i * 256, 256), 256)
-            v = nn(start_t[s, :], cot_first[...]) + nn(later_t[s, :], cot_second[...])
-            IP[it, 0, s, :] = v[:, 0:128]
-            IP[it, 1, s, :] = v[:, 128:256]
-
-        op = copy(IP.at[it, 1 - c], RB.at[it], base, partner)
-        total_step(1 + it, 2)
-        op.wait_recv()
+        swap = []
         for a in range(2):
             rows = slice(768 * a, 768 * a + 768)
-            ACC[it, a] = (IP[it, c, rows, :] + RB[it, rows, :]).reshape(4, 4, 48, 128)
+            v = nn(start_t[rows, :], cot_first[...]) + nn(later_t[rows, :], cot_second[...])
+            keep, give = halves(v, it)
+            IPW[it, a] = give.reshape(4, 4, 48, 128).astype(BF16)
+            swap.append(copy(IPW.at[it, a], RB.at[it, a], base + a, partner))
+            IP[it, a] = keep.reshape(4, 4, 48, 128)
+        total_step(1 + it, 2)
         todo = []
-        for d in (1, 2, 3):
-            todo.append(copy(ACC.at[it, 0, :, (y + d) % 4], R1.at[it, 0, d - 1], base + d, axis_dev("y", d)))
-            todo.append(copy(ACC.at[it, 1, (z + d) % 4], R1.at[it, 1, d - 1], base + 3 + d, axis_dev("z", d)))
+        for a in range(2):
+            swap[a].wait_recv()
+            v = IP[it, a] + RB[it, a].astype(F32)
+            ACC[it, a] = v
+            ACCW[it, a] = v.astype(BF16)
+            for d in (2, 1, 3):
+                if a == 0:
+                    todo.append(
+                        copy(ACCW.at[it, 0, :, (y + d) % 4], R1.at[it, 0, d - 1], base + 1 + d, axis_dev("y", d))
+                    )
+                else:
+                    todo.append(copy(ACCW.at[it, 1, (z + d) % 4], R1.at[it, 1, d - 1], base + 4 + d, axis_dev("z", d)))
         total = whole(total_step(1 + it, 3))
-        for op in todo:
-            op.wait_recv()
-        T2[it, 0] = ACC[it, 0, :, y] + R1[it, 0, 0] + R1[it, 0, 1] + R1[it, 0, 2]
-        T2[it, 1] = ACC[it, 1, z] + R1[it, 1, 0] + R1[it, 1, 1] + R1[it, 1, 2]
+        second_todo = []
+        for a in range(2):
+            for op in todo[3 * a : 3 * a + 3]:
+                op.wait_recv()
+            v = ACC[it, 0, :, y] if a == 0 else ACC[it, 1, z]
+            for d in range(3):
+                v = v + R1[it, a, d].astype(F32)
+            T2[it, a] = v
+            T2W[it, a] = v.astype(BF16)
+            for d in (2, 1, 3):
+                axis, own = ("z", z) if a == 0 else ("y", y)
+                second_todo.append(
+                    copy(T2W.at[it, a, (own + d) % 4], R2.at[it, a, d - 1], base + 7 + 3 * a + d, axis_dev(axis, d))
+                )
+        for a in range(2):
+            for op in second_todo[3 * a : 3 * a + 3]:
+                op.wait_recv()
+            v = T2[it, a, z if a == 0 else y]
+            for d in range(3):
+                v = v + R2[it, a, d].astype(F32)
+            T3[it, x, a] = v.astype(BF16)
         todo = []
-        for d in (1, 2, 3):
-            todo.append(copy(T2.at[it, 0, (z + d) % 4], R2.at[it, 0, d - 1], base + 6 + d, axis_dev("z", d)))
-            todo.append(copy(T2.at[it, 1, (y + d) % 4], R2.at[it, 1, d - 1], base + 9 + d, axis_dev("y", d)))
-        for op in todo:
-            op.wait_recv()
-        T3[it, x, 0] = T2[it, 0, z] + R2[it, 0, 0] + R2[it, 0, 1] + R2[it, 0, 2]
-        T3[it, x, 1] = T2[it, 1, y] + R2[it, 1, 0] + R2[it, 1, 1] + R2[it, 1, 2]
-        todo = []
-        for d in (1, 2, 3):
-            todo.append(copy(T3.at[it, x], T3.at[it, x], base + 12 + d, axis_dev("x", d)))
+        for d in (2, 1, 3):
+            todo.append(copy(T3.at[it, x], T3.at[it, x], base + 13 + d, axis_dev("x", d)))
         for op in todo:
             op.wait_recv()
         return total
 
+    def summed(it, h):
+        v = T3[it, 0, h].astype(F32)
+        for i in range(1, 4):
+            v = v + T3[it, i, h].astype(F32)
+        return v
+
     finish_sweep(0)
     bend = sum_image(0) + DAMPING * rr
     alpha1 = rr / bend
-    image = T3[0, 0] + T3[0, 1] + T3[0, 2] + T3[0, 3]
-    residual = g32[...] - alpha1 * (image + DAMPING * g32[...])
-    res32[...] = residual
-    RG[c, 0, z, y] = residual[0].astype(BF16)
-    RG[c, 1, z, y] = residual[1].astype(BF16)
+    for a in range(2):
+        g = g32[a]
+        residual = g - alpha1 * (summed(0, a) + DAMPING * g)
+        res32[a] = residual
+        RG[c, a, z, y] = residual.astype(BF16)
     todo = []
-    for d in (1, 2, 3):
+    for d in (2, 1, 3):
         ref = RG.at[c, 0, z, y]
-        todo.append(copy(ref, ref, gather_base + d - 1, axis_dev("y", d)))
+        todo.append((d, copy(ref, ref, gather_base + d - 1, axis_dev("y", d))))
         ref = RG.at[c, 1, z, y]
-        todo.append(copy(ref, ref, gather_base + d + 2, axis_dev("z", d)))
-    for op in todo:
+        todo.append((d, copy(ref, ref, gather_base + d + 2, axis_dev("z", d))))
+    for d, op in todo:
         op.wait_recv()
-    todo = []
-    for d in (1, 2, 3):
+    last = []
+    for d in (2, 1, 3):
         ref = RG.at[c, 0, z]
-        todo.append(copy(ref, ref, gather_base + d + 5, axis_dev("z", d)))
+        last.append((0, d, copy(ref, ref, gather_base + d + 5, axis_dev("z", d))))
         ref = RG.at[c, 1, :, y]
-        todo.append(copy(ref, ref, gather_base + d + 8, axis_dev("y", d)))
-    for op in todo:
+        last.append((1, d, copy(ref, ref, gather_base + d + 8, axis_dev("y", d))))
+    swap = [
+        copy(RG.at[c, 0, z], RG.at[c, 0, z], gather_base + 12, partner),
+        copy(RG.at[c, 1, :, y], RG.at[c, 1, :, y], gather_base + 13, partner),
+    ]
+    mine = res32[hi]
+    res_near[...] = jnp.where(c == 0, mine[24:48], mine[0:24])
+    op_res = copy(res_near, res_far, fresh(), partner)
+    for n, (a, d, op) in enumerate(last[2:] + last[:2]):
         op.wait_recv()
-    op = copy(RG.at[c], RG.at[c], gather_base + 12, partner)
-    op.wait_recv()
+        ref = RG.at[c, 0, (z - d + 4) % 4] if a == 0 else RG.at[c, 1, :, (y - d + 4) % 4]
+        swap.append(copy(ref, ref, gather_base + 14 + n, partner))
+    for op in swap:
+        op.wait_recv()
 
     tile = jnp.zeros((8, 128), F32)
     for cc in range(2):
@@ -607,13 +684,13 @@
     tmix[...] = nn(tfirst[...].astype(BF16), embed[...])
     tangent_norm(256)
     for cc in range(2):
-        @pl.loop(0, 6)
+        @pl.loop(0, 6, unroll=True)
         def _(t):
             cols = pl.ds(pl.multiple_of(cc * 1536 + t * 256, 256), 256)
             w = HI[cc, t].reshape(D, 256)
             AA[256:512, cols] = (slope[:, cols] * nn(NT[256:512, :], w)).astype(BF16)
 
-    @pl.loop(0, 6)
+    @pl.loop(0, 6, unroll=True)
     def _(t):
         cols = pl.ds(pl.multiple_of(t * 256, 256), 256)
         w = HO[t].reshape(FF, 256)
@@ -622,39 +699,30 @@
     finish_sweep(1)
     bend = sum_image(1) + DAMPING * dd
     alpha2 = new / bend
-    image = T3[1, 0, hi] + T3[1, 1, hi] + T3[1, 2, hi] + T3[1, 3, hi]
-    g = g32[hi]
-    res = res32[hi]
+    image = summed(1, hi)
+    image = jnp.concatenate([image[0:24], image[24:48]], axis=1)
+    g = gradient[...]
+    op_res.wait_recv()
+    mine = res32[hi]
+    mine = jnp.where(c == 0, mine[0:24], mine[24:48])
+    other = res_far[...]
+    res = jnp.concatenate([jnp.where(c == 0, mine, other), jnp.where(c == 0, other, mine)], axis=1)
     direction = res + beta * g
-    new_update = alpha1 * g + alpha2 * direction
-    new_residual = res - alpha2 * (image + DAMPING * direction)
-    out_near[0] = jnp.where(c == 0, new_update[24:48], new_update[0:24])
-    out_near[1] = jnp.where(c == 0, new_residual[24:48], new_residual[0:24])
-    op = copy(out_near, out_far, fresh(), partner)
-    mine_u = jnp.where(c == 0, new_update[0:24], new_update[24:48])
-    mine_r = jnp.where(c == 0, new_residual[0:24], new_residual[24:48])
-    op.wait_recv()
-    for mine, k, out in ((mine_u, 0, out_update), (mine_r, 1, out_residual)):
-        other = out_far[k]
-        out[:, 0:128] = jnp.where(c == 0, mine, other)
-        out[:, 128:256] = jnp.where(c == 0, other, mine)
+    out_update[...] = alpha1 * g + alpha2 * direction
+    out_residual[...] = res - alpha2 * (image + DAMPING * direction)
     for op in pending:
         op.wait_send()
 
 
 def body(states, policy, action_embed, norm_gain, hidden_in, hidden_out, precision, gradient):
-    wide = policy.astype(F32)
-    gains = jnp.broadcast_to(norm_gain.astype(F32)[:, None], (norm_gain.shape[0], 128))
-    pack = jnp.concatenate(
-        [wide[:, 0:128], gradient[:, 0:128], gains, wide[:, 128:256], gradient[:, 128:256], gains], axis=1
-    )
-    embed = action_embed.reshape(4, 4, 3, 128).transpose(2, 1, 0, 3).reshape(48, 128)
     vmem = pl.BlockSpec(memory_space=pltpu.VMEM)
     shapes = [
         ((2, 3, 2, 4, 4, 64, 128), BF16),
         ((2, 6, 2, 4, 4, 48, 256), BF16),
         ((6, 2, 4, 4, 2, 48, 256), BF16),
+        ((24, 768), F32),
         ((24, 384), F32),
+        ((48, 128), F32),
         ((24, 3072), F32),
         ((24, 1536), F32),
         ((D, ACT), BF16),
@@ -681,26 +749,29 @@
         ((ROWS, FF), BF16),
         ((ROWS, ACT), BF16),
         ((ROWS, ACT), BF16),
-        ((2, 2, D, 128), F32),
-        ((2, D, 128), F32),
         ((2, 2, 4, 4, 48, 128), F32),
-        ((2, 2, 3, 4, 48, 128), F32),
+        ((2, 2, 4, 4, 48, 128), BF16),
+        ((2, 2, 4, 4, 48, 128), BF16),
+        ((2, 2, 4, 4, 48, 128), F32),
+        ((2, 2, 4, 4, 48, 128), BF16),
+        ((2, 2, 3, 4, 48, 128), BF16),
         ((2, 2, 4, 48, 128), F32),
-        ((2, 2, 3, 48, 128), F32),
-        ((2, 4, 2, 48, 128), F32),
+        ((2, 2, 4, 48, 128), BF16),
+        ((2, 2, 3, 48, 128), BF16),
+        ((2, 4, 2, 48, 128), BF16),
         ((3, 4, 4, 8, 128), F32),
         ((2, 48, 128), F32),
         ((2, 48, 128), F32),
         ((2, 2, 4, 4, 48, 128), BF16),
-        ((2, 24, 128), F32),
-        ((2, 24, 128), F32),
+        ((24, 128), F32),
+        ((24, 128), F32),
     ]
     n_sems = N_ITEM * ITEM_SEMS + OTHER_SEMS
     out = jax.ShapeDtypeStruct(gradient.shape, F32)
     return pl.pallas_call(
         kernel,
         out_shape=(out, out),
-        in_specs=[vmem] * 6,
+        in_specs=[vmem] * 8,
         out_specs=(vmem, vmem),
         scratch_shapes=[pltpu.VMEM(s, t) for s, t in shapes]
         + [pltpu.SemaphoreType.DMA((n_sems,)), pltpu.SemaphoreType.DMA((n_sems,))],
@@ -708,7 +779,16 @@
             collective_id=0, has_side_effects=True, vmem_limit_bytes=62 * 2**20
         ),
         name="natural_step",
-    )(states, pack, embed, hidden_in, hidden_out, precision.reshape(1, ACT))
+    )(
+        states,
+        policy,
+        action_embed,
+        norm_gain.reshape(1, -1),
+        hidden_in,
+        hidden_out,
+        precision.reshape(1, ACT),
+        gradient,
+    )
 
 
 def solution(mesh):

time: 160 us -> 135 us (0.84); the launches traced: 158 us -> 135 us
  Pallas kernels: 153 us -> 132 us
  local copies, waits for them, and re-layouts: 4.04 us -> 1.96 us
    pallas_call x1, Pallas kernels: 153 us -> 132 us  [body(): pl.pallas_call(kernel, out_shape=(out, out), in_specs=[vmem] * 8, out_spe...]
    unnamed x17 -> x4, local copies, waits for them, and re-layouts: 3.34 us -> 1.96 us
where the time goes in v2:
time: 135 us
  Pallas kernels  132 us (98%)
  local copies, waits for them, and re-layouts  1.96 us (1%)
    pallas_call x1, Pallas kernels, body(): pl.pallas_call(kernel, out_shape=(out, out), in_specs=[vmem] * 8, out_spe...  132 us

profile of v2, /device:TPU:0, one launch (start us, length us, event | category | flops | bytes accessed | tf_op | source)
XLA Modules:
  0.0 134.8 jit_solution(1956756888885838773)
XLA Ops:
  0.6 132.2 %natural_step.1 = (f32[24,256]{1,0:T(8,128)}, f32[24,256]{1,0:T(8,128)}) custom-call(bf16[256,1536]{1,0:T(8,128)(2,1)} %states.1, bf16[24,256]{1,0:T(8,128)(2,1)} %policy_in.1, bf16[4,1536]{1,0:T(4,128)(2,1)} %embed_in.1, bf16[1,24]{1,0:T(2,128)(2,1)} %bitcast.3, bf16[24,3072]{1,0:T(8,128)(2,1)} %inner_in.1, bf16[48,1536]{1,0:T(8,128)(2,1)} %outer_in.1, ...), custom_call_target="tpu_custom_call" | custom-call | tf_op jit(solution)/shard_map/natural_step/pallas_call | solution.py:771
  132.8 0.0 copy-start
  132.8 1.4 %copy.12 = f32[24,256]{1,0:T(8,128)} copy(f32[24,256]{1,0:T(8,128)} %get-tuple-element.4) | data formatting | bytes 49152
  134.2 0.0 copy-done
  134.2 0.6 copy.13
Async XLA Ops:
  132.8 1.4 %copy-start = (f32[24,256]{1,0:T(8,128)S(1)}, f32[24,256]{1,0:T(8,128)}, u32[]{:S(2)}) copy-start(f32[24,256]{1,0:T(8,128)} %get-tuple-element.5) | copy-start | bytes 73732

commit v3 on v2

--- a/solution.py
+++ b/solution.py
@@ -20,8 +20,8 @@
 ACT = 256
 TOTAL_ROWS = 32768
 N_ITEM = 5
-ITEM_SEMS = 41
-OTHER_SEMS = 2 + 1 + 6 + 30 + 2 * 17 + 20 + 1
+N_SEND = 90
+N_RECV = 124
 
 
 def nn(left, right):
@@ -118,26 +118,34 @@
     opp = ((3 - x) % 2, ((((3 - x) // 2) * 4 + z) * 4 + y) * 2 + c)
     partner = dev(core=1 - c)
 
-    pending = []
-    counter = [N_ITEM * ITEM_SEMS]
-
-    def copy(src, dst, sem, to):
-        op = pltpu.make_async_remote_copy(
+    used = [0, 0]
+    sent = []
+
+    def fresh(which, n=1):
+        used[which] += n
+        assert used[which] <= (N_SEND, N_RECV)[which]
+        return used[which] - n
+
+    def describe(src, dst, s_sem, r_sem, to):
+        return pltpu.make_async_remote_copy(
             src_ref=src,
             dst_ref=dst,
-            send_sem=send_sem.at[sem],
-            recv_sem=recv_sem.at[sem],
+            send_sem=send_sem.at[s_sem],
+            recv_sem=recv_sem.at[r_sem],
             device_id=to,
             device_id_type=MESH,
         )
-        op.start()
-        pending.append(op)
-        return op
-
-    def fresh(n=1):
-        base = counter[0]
-        counter[0] += n
-        return base
+
+    def copy(src, dst, s_sem, r_sem, to):
+        describe(src, dst, s_sem, r_sem, to).start()
+
+    def take(r_sem, ref):
+        describe(ref, ref, 0, r_sem, partner).wait_recv()
+
+    def sending(ref):
+        s_sem = fresh(0)
+        sent.append((s_sem, ref))
+        return s_sem
 
     barrier = pltpu.get_barrier_semaphore()
     peers = [partner] + [axis_dev(a, d) for a in ("x", "y", "z") for d in (1, 2, 3)]
@@ -158,170 +166,172 @@
             embed_near[16 * s + 4 * q : 16 * s + 4 * q + 4, :] = wide[:, column : column + 128]
     pl.semaphore_wait(barrier, len(peers))
 
+    near_half = pl.ds(pl.multiple_of(c * 384, 128), 384)
+    far_half = pl.ds(pl.multiple_of((1 - c) * 384, 128), 384)
+    pack_sem = fresh(1)
+    copy(pack.at[:, far_half], pack_far, sending(pack_far), pack_sem, partner)
     half = pl.ds(pl.multiple_of((1 - c) * 1536, 128), 1536)
-    op_inner = copy(inner_wide.at[:, half], inner_far, fresh(), partner)
-    half = pl.ds(pl.multiple_of((1 - c) * 384, 128), 384)
-    op_pack = copy(pack.at[:, half], pack_far, fresh(), partner)
-
-    def part(item, t, h, zz, yy, cut):
+    inner_sem = fresh(1)
+    copy(inner_wide.at[:, half], inner_far, sending(inner_far), inner_sem, partner)
+
+    def part(item, t, place, core):
+        h, zz, yy, side = place
         if item == 0:
-            rows = pl.ds(pl.multiple_of(lo * 32, 32), 32) if cut == 0 else ALL
-            if cut == 1:
-                rows = pl.ds(pl.multiple_of((1 - lo) * 32, 32), 32)
-            return S.at[c, t, h, zz, yy, rows, :]
-        cols = ALL
-        if cut == 0:
-            cols = pl.ds(pl.multiple_of(lo * 128, 128), 128)
-        if cut == 1:
-            cols = pl.ds(pl.multiple_of((1 - lo) * 128, 128), 128)
+            rows = ALL if side is None else pl.ds(pl.multiple_of(side * 32, 32), 32)
+            return S.at[core, t, h, zz, yy, rows, :]
+        cols = ALL if side is None else pl.ds(pl.multiple_of(side * 128, 128), 128)
         if item < 3:
-            return HI.at[c, (item - 1) * 3 + t, h, zz, yy, :, cols]
-        return HO.at[(item - 3) * 3 + t, h, zz, yy, c, :, cols]
+            return HI.at[core, (item - 1) * 3 + t, h, zz, yy, :, cols]
+        return HO.at[(item - 3) * 3 + t, h, zz, yy, core, :, cols]
 
     one = lambda i: pl.ds(i, 1)
-    ops = {}
-
-    def send(item, key, sem, t, h, zz, yy, cut, to):
-        ref = part(item, t, h, zz, yy, cut)
-        ops[(item, key)] = copy(ref, ref, item * ITEM_SEMS + sem, to)
-
-    def wait(item, *keys):
-        for key in keys:
-            ops[(item, key)].wait_recv()
-
-    def stage_a(k):
-        send(k, "0x", 0, 0, one(hi), one(z), one(y), None, opp)
-        for d in (1, 2, 3):
-            send(k, "1y%d" % d, 8 + d, 1, one(hi), one(z), one(y), 0, axis_dev("y", d))
-            send(k, "2z%d" % d, 18 + d, 2, one(hi), one(z), one(y), None, axis_dev("z", d))
-
-    def stage_b(k):
-        wait(k, "0x")
-        for d in (1, 2, 3):
-            send(k, "0y%d" % d, d, 0, ALL, one(z), one(y), None, axis_dev("y", d))
-        wait(k, "1y1", "1y2", "1y3")
-        for d in (1, 2, 3):
-            send(k, "1z%d" % d, 11 + d, 1, one(hi), one(z), ALL, 0, axis_dev("z", d))
-        wait(k, "2z1", "2z2", "2z3")
-        send(k, "2x", 22, 2, one(hi), ALL, one(y), None, opp)
-
-    def hand(k, key, sem, t, h, zz, yy, cut):
-        send(k, key, 26 + sem, t, h, zz, yy, cut, partner)
-
     low, high = pl.ds(0, 2), pl.ds(2, 2)
     h0, h1 = pl.ds(0, 1), pl.ds(1, 1)
-    zb, zf, zo = (z + 3) % 4, (z + 1) % 4, (z + 2) % 4
-    yb, yf, yo = (y + 3) % 4, (y + 1) % 4, (y + 2) % 4
-
-    def x_part(k, d):
-        xx = (x + d) % 4
-        h = one(xx // 2)
-        other = xx % 2
+    first_two, first_three = pl.ds(0, 2), pl.ds(0, 3)
+    here, zh, yh = one(hi), one(z), one(y)
+    ring_axis = {(0, 2): "y", (0, 3): "z", (1, 2): "z", (1, 3): "x", (2, 2): "x", (2, 3): "y"}
+
+    def piece(t, p, d, sub=None):
+        xx, zd, yd = (x + d) % 4, one((z + d) % 4), one((y + d) % 4)
+        hs = ALL if sub is None else (h0, h1)[sub]
+        pair = ALL if sub is None else (low, high)[sub]
+        return {
+            (0, 2): (hs, zh, yd, None),
+            (0, 3): (hs, zd, ALL, None),
+            (1, 2): (here, zd, pair, lo),
+            (1, 3): (one(xx // 2), pair, ALL, xx % 2),
+            (2, 2): (one(xx // 2), pair, yh, xx % 2),
+            (2, 3): (hs, ALL, yd, None),
+        }[(t, p)]
+
+    two_pieces = {
+        (0, 2): (ALL, zh, first_two, None),
+        (0, 3): (ALL, first_two, ALL, None),
+        (1, 2): (here, first_two, ALL, lo),
+        (1, 3): (here, ALL, ALL, None),
+        (2, 2): (here, ALL, yh, None),
+        (2, 3): (ALL, ALL, first_two, None),
+    }
+    three_pieces = {
+        (0, 2): (ALL, zh, first_three, None),
+        (0, 3): (ALL, first_three, ALL, None),
+        (1, 2): (here, first_three, ALL, lo),
+        (1, 3): (ALL, first_three, ALL, None),
+        (2, 2): (ALL, first_three, yh, None),
+        (2, 3): (ALL, ALL, first_three, None),
+    }
+    recv_of = {}
+    send_of = {}
+
+    def ship(k, t, place, s_sem, r_sem, to):
+        ref = part(k, t, place, c)
+        copy(ref, ref, s_sem, r_sem, to)
+
+    def arrived(k, t, place, key):
+        take(recv_of[key], part(k, t, place, c))
+
+    first_places = (
+        (here, zh, yh, None),
+        (here, zh, first_three, lo),
+        (here, first_three, yh, lo),
+    )
+
+    def stage_a(k):
+        for t in range(3):
+            s_sem = sending(part(k, t, first_places[t], c))
+            recv_of[(k, t, 1)] = r_sem = fresh(1)
+            if t == 0:
+                ship(k, t, (here, zh, yh, None), s_sem, r_sem, opp)
+            else:
+                for d in (1, 3, 2):
+                    ship(k, t, (here, zh, yh, lo), s_sem, r_sem, axis_dev("yz"[t - 1], d))
+
+    def ring_start(k, t, p):
+        axis = ring_axis[(t, p)]
+        s_sem = sending(part(k, t, three_pieces[(t, p)], c))
+        send_of[(k, t, p)] = s_sem
+        base = fresh(1, 2)
+        recv_of[(k, t, p, "near")], recv_of[(k, t, p, "far")] = base, base + 1
+        if p == 3 and k == N_ITEM - 1:
+            recv_of[(k, t, p, "rest")] = rest = fresh(1)
+            for sub, sem in ((0, base), (1, rest)):
+                ship(k, t, piece(t, p, 0, sub), s_sem, sem, axis_dev(axis, 1))
+                ship(k, t, piece(t, p, 0, 1 - sub), s_sem, sem, axis_dev(axis, 3))
+        else:
+            ship(k, t, piece(t, p, 0), s_sem, base, axis_dev(axis, 1))
+            ship(k, t, piece(t, p, 0), s_sem, base, axis_dev(axis, 3))
+
+    def ring_pass(k, t, p):
+        axis = ring_axis[(t, p)]
+        s_sem, r_sem = send_of[(k, t, p)], recv_of[(k, t, p, "far")]
+        place = piece(t, p, 2) if (k, t, p, "rest") in recv_of else two_pieces[(t, p)]
+        arrived(k, t, place, (k, t, p, "near"))
+        ship(k, t, piece(t, p, 3, 0), s_sem, r_sem, axis_dev(axis, 1))
+        ship(k, t, piece(t, p, 1, 1), s_sem, r_sem, axis_dev(axis, 3))
+
+    def item_whole(k, core):
         if k == 0:
-            return h, pl.ds(pl.multiple_of(other * 32, 32), 32), ALL
-        return h, ALL, pl.ds(pl.multiple_of(other * 128, 128), 128)
-
-    def x_ref(k, d, zz):
-        h, rows, cols = x_part(k, d)
-        if k == 0:
-            return S.at[c, 1, h, zz, :, rows, :]
+            return S.at[core]
         if k < 3:
-            return HI.at[c, (k - 1) * 3 + 1, h, zz, :, :, cols]
-        return HO.at[(k - 3) * 3 + 1, h, zz, :, c, :, cols]
-
-    def x_send(k, key, sem, d, zz, to):
-        ref = x_ref(k, d, zz)
-        ops[(k, key)] = copy(ref, ref, k * ITEM_SEMS + sem, to)
-
-    fine_base = fresh(6)
+            return HI.at[core, pl.ds(3 * (k - 1), 3)]
+        return HO.at[pl.ds(3 * (k - 3), 3), :, :, :, core]
+
+    def hand(k, t, d):
+        s_sem, r_sem = send_of[k], recv_of[k]
+        ship(k, t, piece(t, 3, d), s_sem, r_sem, partner)
+
+    def stage_b(k):
+        for t in range(3):
+            arrived(k, t, first_places[t], (k, t, 1))
+            ring_start(k, t, 2)
+
+    def stage_g(k):
+        for t in range(3):
+            ring_pass(k, t, 2)
 
     def stage_c(k):
-        fine = k == N_ITEM - 1
-        f0, b0, fl, bl = (h0, h1, low, high) if fine else (ALL, ALL, ALL, ALL)
-        wait(k, "0y1", "0y2", "0y3")
-        send(k, "0f", 4, 0, f0, one(z), ALL, None, axis_dev("z", 1))
-        send(k, "0b", 5, 0, b0, one(z), ALL, None, axis_dev("z", 3))
-        wait(k, "1z1", "1z2", "1z3")
-        x_send(k, "1f", 15, 0, fl, axis_dev("x", 1))
-        x_send(k, "1b", 16, 0, bl, axis_dev("x", 3))
-        wait(k, "2x")
-        send(k, "2f", 23, 2, f0, ALL, one(y), None, axis_dev("y", 1))
-        send(k, "2b", 24, 2, b0, ALL, one(y), None, axis_dev("y", 3))
-        if fine:
-            sem = fine_base - k * ITEM_SEMS
-            send(k, "0F", sem, 0, h1, one(z), ALL, None, axis_dev("z", 1))
-            send(k, "0B", sem + 1, 0, h0, one(z), ALL, None, axis_dev("z", 3))
-            x_send(k, "1F", sem + 2, 0, high, axis_dev("x", 1))
-            x_send(k, "1B", sem + 3, 0, low, axis_dev("x", 3))
-            send(k, "2F", sem + 4, 2, h1, ALL, one(y), None, axis_dev("y", 1))
-            send(k, "2B", sem + 5, 2, h0, ALL, one(y), None, axis_dev("y", 3))
-        hand(k, "0p0", 0, 0, ALL, one(z), ALL, None)
-        x_send(k, "1p0", 26 + 5, 0, ALL, partner)
-        hand(k, "2p0", 10, 2, ALL, ALL, one(y), None)
+        for t in range(3):
+            arrived(k, t, piece(t, 2, 2), (k, t, 2, "far"))
+            ring_start(k, t, 3)
+        send_of[k] = sending(item_whole(k, c))
+        recv_of[k] = fresh(1)
+        for t in range(3):
+            hand(k, t, 0)
 
     def stage_d(k):
-        fine = k == N_ITEM - 1
-        wait(k, "0f")
-        send(k, "0ff", 6, 0, h0, one(zb), ALL, None, axis_dev("z", 1))
-        wait(k, "0b")
-        send(k, "0bb", 7, 0, h1, one(zf), ALL, None, axis_dev("z", 3))
-        wait(k, "1f")
-        x_send(k, "1ff", 17, 3, low, axis_dev("x", 1))
-        wait(k, "1b")
-        x_send(k, "1bb", 18, 1, high, axis_dev("x", 3))
-        wait(k, "2f")
-        send(k, "2ff", 25, 2, h0, ALL, one(yb), None, axis_dev("y", 1))
-        wait(k, "2b")
-        send(k, "2bb", 8, 2, h1, ALL, one(yf), None, axis_dev("y", 3))
-        if fine:
-            wait(k, "0F", "0B")
-        hand(k, "0p1", 1, 0, ALL, one(zb), ALL, None)
-        hand(k, "0p2", 2, 0, ALL, one(zf), ALL, None)
-        if fine:
-            wait(k, "1F", "1B")
-        x_send(k, "1p1", 26 + 6, 3, ALL, partner)
-        x_send(k, "1p2", 26 + 7, 1, ALL, partner)
-        if fine:
-            wait(k, "2F", "2B")
-        hand(k, "2p1", 11, 2, ALL, ALL, one(yb), None)
-        hand(k, "2p2", 12, 2, ALL, ALL, one(yf), None)
+        for t in range(3):
+            ring_pass(k, t, 3)
+        for t in range(3):
+            if (k, t, 3, "rest") in recv_of:
+                arrived(k, t, piece(t, 3, 2), (k, t, 3, "rest"))
+            hand(k, t, 3)
+            hand(k, t, 1)
 
     def stage_e(k):
-        wait(k, "0ff")
-        hand(k, "0p3", 3, 0, h0, one(zo), ALL, None)
-        wait(k, "0bb")
-        hand(k, "0p4", 4, 0, h1, one(zo), ALL, None)
-        wait(k, "1ff")
-        x_send(k, "1p3", 26 + 8, 2, low, partner)
-        wait(k, "1bb")
-        x_send(k, "1p4", 26 + 9, 2, high, partner)
-        wait(k, "2ff")
-        hand(k, "2p3", 13, 2, h0, ALL, one(yo), None)
-        wait(k, "2bb")
-        hand(k, "2p4", 14, 2, h1, ALL, one(yo), None)
+        for t in range(3):
+            arrived(k, t, piece(t, 3, 2), (k, t, 3, "far"))
+            hand(k, t, 2)
 
     def stage_f(k):
-        wait(k, *["%dp%d" % (t, i) for t in range(3) for i in range(5)])
-
-    scalar_ops = {}
-    scalar_base = fresh(30)
+        take(recv_of[k], item_whole(k, 1 - c))
+
+    scalar_sems = {}
     places = (("core", c, 2), ("y", y, 4), ("z", z, 4), ("x", x, 4))
 
     def total_send(which, phase, value):
         axis, own, n = places[phase]
         SC[which, phase, own] = value
         ref = SC.at[which, phase, own]
-        base = scalar_base + 10 * which + (0, 1, 4, 7)[phase]
-        todo = []
+        others = SC.at[which, phase, pl.ds(0, n - 1)]
+        s_sem = sending(others)
+        scalar_sems[(which, phase)] = r_sem = fresh(1)
         for d in range(1, n):
             to = partner if axis == "core" else axis_dev(axis, d)
-            todo.append(copy(ref, ref, base + d - 1, to))
-        scalar_ops[(which, phase)] = todo
+            copy(ref, ref, s_sem, r_sem, to)
 
     def total_take(which, phase):
-        for op in scalar_ops[(which, phase)]:
-            op.wait_recv()
         n = places[phase][2]
+        take(scalar_sems[(which, phase)], SC.at[which, phase, pl.ds(0, n - 1)])
         value = SC[which, phase, 0]
         for i in range(1, n):
             value = value + SC[which, phase, i]
@@ -345,7 +355,7 @@
 
     weigh_rows = outer_in
     for ct in range(6):
-        if ct % 3 == 1:
+        if ct % 3:
             left = weigh_rows[:, 256 * ct : 256 * ct + 128]
             right = weigh_rows[:, 256 * ct + 128 : 256 * ct + 256]
             HO[ct, hi, z, y, c, :, pl.ds(pl.multiple_of(lo * 128, 128), 128)] = jnp.where(lo == 0, left, right)
@@ -354,10 +364,10 @@
 
     stage_a(3)
     stage_a(4)
-    near = pack[:, pl.ds(pl.multiple_of(c * 384, 128), 384)]
+    near = pack[:, near_half]
     g_own = gradient[...]
     total_send(0, 0, fold(g_own * g_own))
-    op_pack.wait_recv()
+    take(pack_sem, pack_far)
     far = pack_far[...]
     pair = jnp.concatenate([jnp.where(c == 0, near, far), jnp.where(c == 0, far, near)], axis=0)
     g32[hi] = pair[:, 128:256]
@@ -367,17 +377,18 @@
     gb = pair[:, 128:256]
     both = jnp.concatenate([gb, pair[16:32, 256:384]], axis=0)
     S[c, 1, hi, z, y, pl.ds(pl.multiple_of(lo * 32, 32), 32)] = jnp.where(lo == 0, both[0:32], both[32:64]).astype(BF16)
-    S[c, 2, hi, z, y, 0:48] = embed_near[...].astype(BF16)
-    S[c, 2, hi, z, y, 48:64] = gains[32:48]
+    both = jnp.concatenate([embed_near[...], pair[32:48, 256:384]], axis=0)
+    S[c, 2, hi, z, y, pl.ds(pl.multiple_of(lo * 32, 32), 32)] = jnp.where(lo == 0, both[0:32], both[32:64]).astype(BF16)
     stage_a(0)
-    op_g32 = copy(g32.at[one(hi)], g32.at[one(hi)], fresh(), opp)
-
-    op_inner.wait_recv()
+    g_sem = fresh(1)
+    copy(g32.at[hi], g32.at[hi], sending(g32.at[hi]), g_sem, opp)
+
+    take(inner_sem, inner_far)
     near = inner_wide[:, pl.ds(pl.multiple_of(c * 1536, 128), 1536)]
     far = inner_far[...]
     pair = jnp.concatenate([jnp.where(c == 0, near, far), jnp.where(c == 0, far, near)], axis=0)
     for ct in range(6):
-        if ct % 3 == 1:
+        if ct % 3:
             left = pair[:, 256 * ct : 256 * ct + 128]
             right = pair[:, 256 * ct + 128 : 256 * ct + 256]
             HI[c, ct, hi, z, y, :, pl.ds(pl.multiple_of(lo * 128, 128), 128)] = jnp.where(lo == 0, left, right).astype(BF16)
@@ -386,13 +397,18 @@
     stage_a(1)
     stage_a(2)
     stage_b(3)
+    stage_b(4)
     stage_b(0)
     stage_b(1)
+    stage_b(2)
+    stage_g(3)
+    stage_g(4)
+    stage_g(0)
+    stage_g(1)
     stage_c(0)
+    stage_g(2)
     total_step(0, 0)
-    stage_b(2)
     stage_c(1)
-    stage_b(4)
     total_step(0, 1)
     stage_d(0)
 
@@ -507,7 +523,7 @@
     stage_e(4)
     stage_f(4)
     take_outer(1)
-    op_g32.wait_recv()
+    take(g_sem, g32.at[1 - hi])
 
     second = jnp.tanh(nn(later[...], policy[...]))
     second_d[...] = 1.0 - second * second
@@ -557,9 +573,6 @@
         cf = (first_d[...] * (weighting * tfirst[...] + nt(cot_b[...], embed[...]))).astype(BF16)
         cot_first[...] = cf
 
-    r_base = [fresh(17), fresh(17)]
-    gather_base = fresh(20)
-
     def halves(v, it):
         if it == 0:
             low_half, high_half = v[:, 0:128], v[:, 128:256]
@@ -571,56 +584,54 @@
         return jnp.where(c == 0, low_half, high_half), jnp.where(c == 0, high_half, low_half)
 
     def sum_image(it):
-        base = r_base[it]
         swap = []
         for a in range(2):
             rows = slice(768 * a, 768 * a + 768)
             v = nn(start_t[rows, :], cot_first[...]) + nn(later_t[rows, :], cot_second[...])
             keep, give = halves(v, it)
             IPW[it, a] = give.reshape(4, 4, 48, 128).astype(BF16)
-            swap.append(copy(IPW.at[it, a], RB.at[it, a], base + a, partner))
+            swap.append(fresh(1))
+            copy(IPW.at[it, a], RB.at[it, a], sending(IPW.at[it, a]), swap[a], partner)
             IP[it, a] = keep.reshape(4, 4, 48, 128)
         total_step(1 + it, 2)
-        todo = []
+        sems = []
         for a in range(2):
-            swap[a].wait_recv()
+            take(swap[a], RB.at[it, a])
             v = IP[it, a] + RB[it, a].astype(F32)
             ACC[it, a] = v
             ACCW[it, a] = v.astype(BF16)
+            s_sem = sending(R1.at[it, a])
+            sems.append(fresh(1))
             for d in (2, 1, 3):
                 if a == 0:
-                    todo.append(
-                        copy(ACCW.at[it, 0, :, (y + d) % 4], R1.at[it, 0, d - 1], base + 1 + d, axis_dev("y", d))
-                    )
+                    copy(ACCW.at[it, 0, :, (y + d) % 4], R1.at[it, 0, d - 1], s_sem, sems[a], axis_dev("y", d))
                 else:
-                    todo.append(copy(ACCW.at[it, 1, (z + d) % 4], R1.at[it, 1, d - 1], base + 4 + d, axis_dev("z", d)))
+                    copy(ACCW.at[it, 1, (z + d) % 4], R1.at[it, 1, d - 1], s_sem, sems[a], axis_dev("z", d))
         total = whole(total_step(1 + it, 3))
-        second_todo = []
+        second_sems = []
         for a in range(2):
-            for op in todo[3 * a : 3 * a + 3]:
-                op.wait_recv()
+            take(sems[a], R1.at[it, a])
             v = ACC[it, 0, :, y] if a == 0 else ACC[it, 1, z]
             for d in range(3):
                 v = v + R1[it, a, d].astype(F32)
             T2[it, a] = v
             T2W[it, a] = v.astype(BF16)
+            s_sem = sending(R2.at[it, a])
+            second_sems.append(fresh(1))
+            axis, own = ("z", z) if a == 0 else ("y", y)
             for d in (2, 1, 3):
-                axis, own = ("z", z) if a == 0 else ("y", y)
-                second_todo.append(
-                    copy(T2W.at[it, a, (own + d) % 4], R2.at[it, a, d - 1], base + 7 + 3 * a + d, axis_dev(axis, d))
-                )
+                copy(T2W.at[it, a, (own + d) % 4], R2.at[it, a, d - 1], s_sem, second_sems[a], axis_dev(axis, d))
         for a in range(2):
-            for op in second_todo[3 * a : 3 * a + 3]:
-                op.wait_recv()
+            take(second_sems[a], R2.at[it, a])
             v = T2[it, a, z if a == 0 else y]
             for d in range(3):
                 v = v + R2[it, a, d].astype(F32)
             T3[it, x, a] = v.astype(BF16)
-        todo = []
+        three = T3.at[it, pl.ds(0, 3)]
+        s_sem, r_sem = sending(three), fresh(1)
         for d in (2, 1, 3):
-            todo.append(copy(T3.at[it, x], T3.at[it, x], base + 13 + d, axis_dev("x", d)))
-        for op in todo:
-            op.wait_recv()
+            copy(T3.at[it, x], T3.at[it, x], s_sem, r_sem, axis_dev("x", d))
+        take(r_sem, three)
         return total
 
     def summed(it, h):
@@ -637,33 +648,34 @@
         residual = g - alpha1 * (summed(0, a) + DAMPING * g)
         res32[a] = residual
         RG[c, a, z, y] = residual.astype(BF16)
-    todo = []
+    three = (RG.at[c, 0, z, first_three], RG.at[c, 1, first_three, y])
+    sems = (fresh(1), fresh(1))
+    s_sems = (sending(three[0]), sending(three[1]))
     for d in (2, 1, 3):
         ref = RG.at[c, 0, z, y]
-        todo.append((d, copy(ref, ref, gather_base + d - 1, axis_dev("y", d))))
+        copy(ref, ref, s_sems[0], sems[0], axis_dev("y", d))
         ref = RG.at[c, 1, z, y]
-        todo.append((d, copy(ref, ref, gather_base + d + 2, axis_dev("z", d))))
-    for d, op in todo:
-        op.wait_recv()
-    last = []
-    for d in (2, 1, 3):
-        ref = RG.at[c, 0, z]
-        last.append((0, d, copy(ref, ref, gather_base + d + 5, axis_dev("z", d))))
-        ref = RG.at[c, 1, :, y]
-        last.append((1, d, copy(ref, ref, gather_base + d + 8, axis_dev("y", d))))
-    swap = [
-        copy(RG.at[c, 0, z], RG.at[c, 0, z], gather_base + 12, partner),
-        copy(RG.at[c, 1, :, y], RG.at[c, 1, :, y], gather_base + 13, partner),
-    ]
+        copy(ref, ref, s_sems[1], sems[1], axis_dev("z", d))
+    swap_send, swap_recv = sending(RG.at[c]), fresh(1)
+    s_sems = (sending(RG.at[c, 0, first_three]), sending(RG.at[c, 1, :, first_three]))
+    last = {}
+    for a in range(2):
+        take(sems[a], three[a])
+        ref = RG.at[c, 0, z] if a == 0 else RG.at[c, 1, :, y]
+        for d in (2, 1, 3):
+            last[(a, d)] = fresh(1)
+            copy(ref, ref, s_sems[a], last[(a, d)], axis_dev("zy"[a], d))
+        copy(ref, ref, swap_send, swap_recv, partner)
     mine = res32[hi]
     res_near[...] = jnp.where(c == 0, mine[24:48], mine[0:24])
-    op_res = copy(res_near, res_far, fresh(), partner)
-    for n, (a, d, op) in enumerate(last[2:] + last[:2]):
-        op.wait_recv()
-        ref = RG.at[c, 0, (z - d + 4) % 4] if a == 0 else RG.at[c, 1, :, (y - d + 4) % 4]
-        swap.append(copy(ref, ref, gather_base + 14 + n, partner))
-    for op in swap:
-        op.wait_recv()
+    res_sem = fresh(1)
+    copy(res_near, res_far, sending(res_near), res_sem, partner)
+    for d in (1, 3, 2):
+        for a in range(2):
+            ref = RG.at[c, 0, (z - d + 4) % 4] if a == 0 else RG.at[c, 1, :, (y - d + 4) % 4]
+            take(last[(a, d)], ref)
+            copy(ref, ref, swap_send, swap_recv, partner)
+    take(swap_recv, RG.at[1 - c])
 
     tile = jnp.zeros((8, 128), F32)
     for cc in range(2):
@@ -702,7 +714,7 @@
     image = summed(1, hi)
     image = jnp.concatenate([image[0:24], image[24:48]], axis=1)
     g = gradient[...]
-    op_res.wait_recv()
+    take(res_sem, res_far)
     mine = res32[hi]
     mine = jnp.where(c == 0, mine[0:24], mine[24:48])
     other = res_far[...]
@@ -710,8 +722,8 @@
     direction = res + beta * g
     out_update[...] = alpha1 * g + alpha2 * direction
     out_residual[...] = res - alpha2 * (image + DAMPING * direction)
-    for op in pending:
-        op.wait_send()
+    for s_sem, ref in sent:
+        describe(ref, ref, s_sem, 0, partner).wait_send()
 
 
 def body(states, policy, action_embed, norm_gain, hidden_in, hidden_out, precision, gradient):
@@ -766,7 +778,6 @@
         ((24, 128), F32),
         ((24, 128), F32),
     ]
-    n_sems = N_ITEM * ITEM_SEMS + OTHER_SEMS
     out = jax.ShapeDtypeStruct(gradient.shape, F32)
     return pl.pallas_call(
         kernel,
@@ -774,7 +785,7 @@
         in_specs=[vmem] * 8,
         out_specs=(vmem, vmem),
         scratch_shapes=[pltpu.VMEM(s, t) for s, t in shapes]
-        + [pltpu.SemaphoreType.DMA((n_sems,)), pltpu.SemaphoreType.DMA((n_sems,))],
+        + [pltpu.SemaphoreType.DMA((N_SEND,)), pltpu.SemaphoreType.DMA((N_RECV,))],
         compiler_params=pltpu.CompilerParams(
             collective_id=0, has_side_effects=True, vmem_limit_bytes=62 * 2**20
         ),

time: 135 us -> 129 us (0.956)
  Pallas kernels: 132 us -> 126 us
    pallas_call x1, Pallas kernels: 132 us -> 126 us  [body(): pl.pallas_call(kernel, out_shape=(out, out), in_specs=[vmem] * 8, out_spe...]
where the time goes in v3:
time: 129 us
  Pallas kernels  126 us (98%)
  local copies, waits for them, and re-layouts  1.96 us (2%)
    pallas_call x1, Pallas kernels, body(): pl.pallas_call(kernel, out_shape=(out, out), in_specs=[vmem] * 8, out_spe...  126 us

profile of v3, /device:TPU:0, one launch (start us, length us, event | category | flops | bytes accessed | tf_op | source)
XLA Modules:
  0.0 129.0 jit_solution(6075910177814932982)
XLA Ops:
  0.6 126.4 %natural_step.1 = (f32[24,256]{1,0:T(8,128)}, f32[24,256]{1,0:T(8,128)}) custom-call(bf16[256,1536]{1,0:T(8,128)(2,1)} %states.1, bf16[24,256]{1,0:T(8,128)(2,1)} %policy_in.1, bf16[4,1536]{1,0:T(4,128)(2,1)} %embed_in.1, bf16[1,24]{1,0:T(2,128)(2,1)} %bitcast.3, bf16[24,3072]{1,0:T(8,128)(2,1)} %inner_in.1, bf16[48,1536]{1,0:T(8,128)(2,1)} %outer_in.1, ...), custom_call_target="tpu_custom_call" | custom-call | tf_op jit(solution)/shard_map/natural_step/pallas_call | solution.py:782
  127.0 0.0 copy-start
  127.0 1.4 %copy.12 = f32[24,256]{1,0:T(8,128)} copy(f32[24,256]{1,0:T(8,128)} %get-tuple-element.4) | data formatting | bytes 49152
  128.4 0.0 copy-done
  128.4 0.6 copy.13
Async XLA Ops:
  127.0 1.4 %copy-start = (f32[24,256]{1,0:T(8,128)S(1)}, f32[24,256]{1,0:T(8,128)}, u32[]{:S(2)}) copy-start(f32[24,256]{1,0:T(8,128)} %get-tuple-element.5) | copy-start | bytes 73732

commit v4 on v3

--- a/solution.py
+++ b/solution.py
@@ -45,8 +45,7 @@
     outer_in,
     precision,
     gradient,
-    out_update,
-    out_residual,
+    out,
     S,
     HI,
     HO,
@@ -298,9 +297,13 @@
         for t in range(3):
             hand(k, t, 0)
 
-    def stage_d(k):
+    def stage_pass(k):
         for t in range(3):
             ring_pass(k, t, 3)
+
+    def stage_d(k):
+        if k < N_ITEM - 1:
+            stage_pass(k)
         for t in range(3):
             if (k, t, 3, "rest") in recv_of:
                 arrived(k, t, piece(t, 3, 2), (k, t, 3, "rest"))
@@ -380,6 +383,7 @@
     both = jnp.concatenate([embed_near[...], pair[32:48, 256:384]], axis=0)
     S[c, 2, hi, z, y, pl.ds(pl.multiple_of(lo * 32, 32), 32)] = jnp.where(lo == 0, both[0:32], both[32:64]).astype(BF16)
     stage_a(0)
+    stage_b(3)
     g_sem = fresh(1)
     copy(g32.at[hi], g32.at[hi], sending(g32.at[hi]), g_sem, opp)
 
@@ -396,28 +400,30 @@
             HI[c, ct, hi, z, y] = pair[:, 256 * ct : 256 * ct + 256].astype(BF16)
     stage_a(1)
     stage_a(2)
-    stage_b(3)
+    stage_g(3)
+    stage_b(0)
+    stage_c(3)
+    stage_b(1)
     stage_b(4)
-    stage_b(0)
-    stage_b(1)
+    stage_g(0)
     stage_b(2)
-    stage_g(3)
-    stage_g(4)
-    stage_g(0)
+    stage_c(0)
     stage_g(1)
-    stage_c(0)
-    stage_g(2)
     total_step(0, 0)
     stage_c(1)
+    stage_d(3)
+    stage_g(2)
+    stage_g(4)
     total_step(0, 1)
     stage_d(0)
+    stage_c(2)
 
     @pl.loop(0, 6)
     def _(i):
         s = pl.ds(pl.multiple_of(i * 256, 256), 256)
         start_t[s, :] = states[:, s].astype(F32).T.astype(BF16)
 
-    stage_c(2)
+    stage_e(3)
     stage_e(0)
     total_step(0, 2)
     stage_f(0)
@@ -451,7 +457,7 @@
         return pl.loop(0, ROWS // n)
 
     stage_d(1)
-    stage_c(3)
+    stage_c(4)
 
     first = jnp.tanh(nn(states[...], policy[...]))
     first_d[...] = 1.0 - first * first
@@ -483,29 +489,28 @@
     tangent_norm(256)
 
     stage_e(1)
+    stage_f(1)
+
+    def take_inner(ch, cc):
+        @pl.loop(0, 3, unroll=True)
+        def _(t):
+            w = HI[cc, ch * 3 + t].reshape(D, 256)
+            cols = pl.ds(pl.multiple_of(cc * 1536 + ch * 768 + t * 256, 256), 256)
+            pre = nn(NT[0:256, :], w)
+            sigma = jax.nn.sigmoid(pre)
+            AA[0:256, cols] = (pre * sigma).astype(BF16)
+            sl = swish_slope(pre, sigma)
+            slope[:, cols] = sl
+            AA[256:512, cols] = (sl * nn(NT[256:512, :], w)).astype(BF16)
+
+    take_inner(0, 0)
     stage_d(2)
-    stage_c(4)
-    stage_f(1)
-
-    def take_inner(ch):
-        for cc in range(2):
-            @pl.loop(0, 3, unroll=True)
-            def _(t):
-                w = HI[cc, ch * 3 + t].reshape(D, 256)
-                cols = pl.ds(pl.multiple_of(cc * 1536 + ch * 768 + t * 256, 256), 256)
-                pre = nn(NT[0:256, :], w)
-                sigma = jax.nn.sigmoid(pre)
-                AA[0:256, cols] = (pre * sigma).astype(BF16)
-                sl = swish_slope(pre, sigma)
-                slope[:, cols] = sl
-                AA[256:512, cols] = (sl * nn(NT[256:512, :], w)).astype(BF16)
-
-    take_inner(0)
+    take_inner(0, 1)
     stage_e(2)
-    stage_d(3)
     stage_f(2)
-    take_inner(1)
-    stage_e(3)
+    take_inner(1, 0)
+    stage_pass(4)
+    take_inner(1, 1)
     stage_d(4)
     stage_f(3)
 
@@ -720,8 +725,8 @@
     other = res_far[...]
     res = jnp.concatenate([jnp.where(c == 0, mine, other), jnp.where(c == 0, other, mine)], axis=1)
     direction = res + beta * g
-    out_update[...] = alpha1 * g + alpha2 * direction
-    out_residual[...] = res - alpha2 * (image + DAMPING * direction)
+    out[0:24, :] = alpha1 * g + alpha2 * direction
+    out[24:48, :] = res - alpha2 * (image + DAMPING * direction)
     for s_sem, ref in sent:
         describe(ref, ref, s_sem, 0, partner).wait_send()
 
@@ -778,12 +783,11 @@
         ((24, 128), F32),
         ((24, 128), F32),
     ]
-    out = jax.ShapeDtypeStruct(gradient.shape, F32)
-    return pl.pallas_call(
+    both = pl.pallas_call(
         kernel,
-        out_shape=(out, out),
+        out_shape=jax.ShapeDtypeStruct((48, ACT), F32),
         in_specs=[vmem] * 8,
-        out_specs=(vmem, vmem),
+        out_specs=vmem,
         scratch_shapes=[pltpu.VMEM(s, t) for s, t in shapes]
         + [pltpu.SemaphoreType.DMA((N_SEND,)), pltpu.SemaphoreType.DMA((N_RECV,))],
         compiler_params=pltpu.CompilerParams(
@@ -800,6 +804,7 @@
         precision.reshape(1, ACT),
         gradient,
     )
+    return both[0:24], both[24:48]
 
 
 def solution(mesh):

time: 129 us -> 139 us (1.078)
  Pallas kernels: 126 us -> 137 us
    pallas_call x1, Pallas kernels: 126 us -> 137 us  [body(): pl.pallas_call(kernel, out_shape=jax.ShapeDtypeStruct((48, ACT), F32), in...]
    unnamed x4 -> x0, local copies, waits for them, and re-layouts: 1.96 us -> none
where the time goes in v4:
time: 139 us
  Pallas kernels  137 us (99%)
    pallas_call x1, Pallas kernels, body(): pl.pallas_call(kernel, out_shape=jax.ShapeDtypeStruct((48, ACT), F32), in...  137 us

profile of v4, /device:TPU:0, one launch (start us, length us, event | category | flops | bytes accessed | tf_op | source)
XLA Modules:
  0.0 138.6 jit_solution(14534071845171955110)
XLA Ops:
  0.6 136.5 %natural_step.1 = f32[48,256]{1,0:T(8,128)} custom-call(bf16[256,1536]{1,0:T(8,128)(2,1)} %states.1, bf16[24,256]{1,0:T(8,128)(2,1)} %policy_in.1, bf16[4,1536]{1,0:T(4,128)(2,1)} %embed_in.1, bf16[1,24]{1,0:T(2,128)(2,1)} %bitcast.3, bf16[24,3072]{1,0:T(8,128)(2,1)} %inner_in.1, bf16[48,1536]{1,0:T(8,128)(2,1)} %outer_in.1, f32[1,256]{1,0:T(1,128)} %bitcast.2, ...), custom_call_target="tpu_custom_call" | custom-call | tf_op jit(solution)/shard_map/natural_step/pallas_call | solution.py:786
  137.2 1.4 fusion

commit v5 on v4

--- a/solution.py
+++ b/solution.py
@@ -19,7 +19,7 @@
 FF = 3072
 ACT = 256
 TOTAL_ROWS = 32768
-N_ITEM = 5
+LAST = 4
 N_SEND = 90
 N_RECV = 124
 
@@ -179,9 +179,9 @@
             rows = ALL if side is None else pl.ds(pl.multiple_of(side * 32, 32), 32)
             return S.at[core, t, h, zz, yy, rows, :]
         cols = ALL if side is None else pl.ds(pl.multiple_of(side * 128, 128), 128)
-        if item < 3:
-            return HI.at[core, (item - 1) * 3 + t, h, zz, yy, :, cols]
-        return HO.at[(item - 3) * 3 + t, h, zz, yy, core, :, cols]
+        if item == 1:
+            return HI.at[core, :, t, h, zz, yy, :, cols]
+        return HO.at[ALL if item == 2 else item - 3, t, h, zz, yy, core, :, cols]
 
     one = lambda i: pl.ds(i, 1)
     low, high = pl.ds(0, 2), pl.ds(2, 2)
@@ -251,7 +251,7 @@
         send_of[(k, t, p)] = s_sem
         base = fresh(1, 2)
         recv_of[(k, t, p, "near")], recv_of[(k, t, p, "far")] = base, base + 1
-        if p == 3 and k == N_ITEM - 1:
+        if p == 3 and k == LAST:
             recv_of[(k, t, p, "rest")] = rest = fresh(1)
             for sub, sem in ((0, base), (1, rest)):
                 ship(k, t, piece(t, p, 0, sub), s_sem, sem, axis_dev(axis, 1))
@@ -271,13 +271,13 @@
     def item_whole(k, core):
         if k == 0:
             return S.at[core]
-        if k < 3:
-            return HI.at[core, pl.ds(3 * (k - 1), 3)]
-        return HO.at[pl.ds(3 * (k - 3), 3), :, :, :, core]
+        if k == 1:
+            return HI.at[core]
+        return HO.at[k - 3, :, :, :, :, core]
 
     def hand(k, t, d):
-        s_sem, r_sem = send_of[k], recv_of[k]
-        ship(k, t, piece(t, 3, d), s_sem, r_sem, partner)
+        if k == 1 or k == LAST:
+            ship(k, t, piece(t, 3, d), send_of[k], recv_of[k], partner)
 
     def stage_b(k):
         for t in range(3):
@@ -290,7 +290,9 @@
 
     def stage_c(k):
         for t in range(3):
-            arrived(k, t, piece(t, 2, 2), (k, t, 2, "far"))
+            if k < LAST:
+                first_two_phases = min(k, 2)
+                arrived(first_two_phases, t, piece(t, 2, 2), (first_two_phases, t, 2, "far"))
             ring_start(k, t, 3)
         send_of[k] = sending(item_whole(k, c))
         recv_of[k] = fresh(1)
@@ -302,8 +304,6 @@
             ring_pass(k, t, 3)
 
     def stage_d(k):
-        if k < N_ITEM - 1:
-            stage_pass(k)
         for t in range(3):
             if (k, t, 3, "rest") in recv_of:
                 arrived(k, t, piece(t, 3, 2), (k, t, 3, "rest"))
@@ -314,6 +314,10 @@
         for t in range(3):
             arrived(k, t, piece(t, 3, 2), (k, t, 3, "far"))
             hand(k, t, 2)
+        if k == 0:
+            copy(S.at[c], S.at[c], send_of[k], recv_of[k], partner)
+        if k == 3:
+            copy(item_whole(k, c), item_whole(k, c), send_of[k], recv_of[k], partner)
 
     def stage_f(k):
         take(recv_of[k], item_whole(k, 1 - c))
@@ -361,12 +365,11 @@
         if ct % 3:
             left = weigh_rows[:, 256 * ct : 256 * ct + 128]
             right = weigh_rows[:, 256 * ct + 128 : 256 * ct + 256]
-            HO[ct, hi, z, y, c, :, pl.ds(pl.multiple_of(lo * 128, 128), 128)] = jnp.where(lo == 0, left, right)
+            HO[ct // 3, ct % 3, hi, z, y, c, :, pl.ds(pl.multiple_of(lo * 128, 128), 128)] = jnp.where(lo == 0, left, right)
         else:
-            HO[ct, hi, z, y, c] = weigh_rows[:, 256 * ct : 256 * ct + 256]
-
-    stage_a(3)
-    stage_a(4)
+            HO[ct // 3, ct % 3, hi, z, y, c] = weigh_rows[:, 256 * ct : 256 * ct + 256]
+
+    stage_a(2)
     near = pack[:, near_half]
     g_own = gradient[...]
     total_send(0, 0, fold(g_own * g_own))
@@ -383,7 +386,6 @@
     both = jnp.concatenate([embed_near[...], pair[32:48, 256:384]], axis=0)
     S[c, 2, hi, z, y, pl.ds(pl.multiple_of(lo * 32, 32), 32)] = jnp.where(lo == 0, both[0:32], both[32:64]).astype(BF16)
     stage_a(0)
-    stage_b(3)
     g_sem = fresh(1)
     copy(g32.at[hi], g32.at[hi], sending(g32.at[hi]), g_sem, opp)
 
@@ -395,35 +397,28 @@
         if ct % 3:
             left = pair[:, 256 * ct : 256 * ct + 128]
             right = pair[:, 256 * ct + 128 : 256 * ct + 256]
-            HI[c, ct, hi, z, y, :, pl.ds(pl.multiple_of(lo * 128, 128), 128)] = jnp.where(lo == 0, left, right).astype(BF16)
+            HI[c, ct // 3, ct % 3, hi, z, y, :, pl.ds(pl.multiple_of(lo * 128, 128), 128)] = jnp.where(lo == 0, left, right).astype(BF16)
         else:
-            HI[c, ct, hi, z, y] = pair[:, 256 * ct : 256 * ct + 256].astype(BF16)
+            HI[c, ct // 3, ct % 3, hi, z, y] = pair[:, 256 * ct : 256 * ct + 256].astype(BF16)
     stage_a(1)
-    stage_a(2)
-    stage_g(3)
+    stage_b(2)
     stage_b(0)
-    stage_c(3)
     stage_b(1)
-    stage_b(4)
+    stage_g(2)
     stage_g(0)
-    stage_b(2)
+    stage_g(1)
     stage_c(0)
-    stage_g(1)
+    stage_c(1)
     total_step(0, 0)
-    stage_c(1)
-    stage_d(3)
-    stage_g(2)
-    stage_g(4)
+    stage_pass(0)
     total_step(0, 1)
-    stage_d(0)
-    stage_c(2)
 
     @pl.loop(0, 6)
     def _(i):
         s = pl.ds(pl.multiple_of(i * 256, 256), 256)
         start_t[s, :] = states[:, s].astype(F32).T.astype(BF16)
 
-    stage_e(3)
+    stage_c(3)
     stage_e(0)
     total_step(0, 2)
     stage_f(0)
@@ -456,6 +451,7 @@
     def blocks(n):
         return pl.loop(0, ROWS // n)
 
+    stage_pass(1)
     stage_d(1)
     stage_c(4)
 
@@ -489,12 +485,13 @@
     tangent_norm(256)
 
     stage_e(1)
+    stage_pass(3)
     stage_f(1)
 
     def take_inner(ch, cc):
         @pl.loop(0, 3, unroll=True)
         def _(t):
-            w = HI[cc, ch * 3 + t].reshape(D, 256)
+            w = HI[cc, ch, t].reshape(D, 256)
             cols = pl.ds(pl.multiple_of(cc * 1536 + ch * 768 + t * 256, 256), 256)
             pre = nn(NT[0:256, :], w)
             sigma = jax.nn.sigmoid(pre)
@@ -504,10 +501,8 @@
             AA[256:512, cols] = (sl * nn(NT[256:512, :], w)).astype(BF16)
 
     take_inner(0, 0)
-    stage_d(2)
     take_inner(0, 1)
-    stage_e(2)
-    stage_f(2)
+    stage_e(3)
     take_inner(1, 0)
     stage_pass(4)
     take_inner(1, 1)
@@ -517,7 +512,7 @@
     def take_outer(ch):
         @pl.loop(0, 3, unroll=True)
         def _(t):
-            w = HO[ch * 3 + t].reshape(FF, 256)
+            w = HO[ch, t].reshape(FF, 256)
             cols = pl.ds(pl.multiple_of(ch * 768 + t * 256, 256), 256)
             l = (mixed[:, cols] + nn(AA[0:256, :], w)).astype(BF16)
             later[:, cols] = l
@@ -549,7 +544,7 @@
             a, b = i // 2, i % 2
             acc = jnp.zeros((ROWS, 768), F32)
             for ct in range(6):
-                w = HO[ct, a, pl.ds(b * 2, 2)].reshape(768, 256)
+                w = HO[ct // 3, ct % 3, a, pl.ds(b * 2, 2)].reshape(768, 256)
                 acc = acc + nt(cot_b[:, 256 * ct : 256 * ct + 256], w)
             cols = pl.ds(pl.multiple_of(i * 768, 256), 768)
             cot_pre[:, cols] = (slope[:, cols] * acc).astype(BF16)
@@ -560,7 +555,7 @@
         def _(a):
             acc = jnp.zeros((ROWS, 768), F32)
             for n in range(12):
-                w = HI[n // 6, n % 6, a].reshape(768, 256)
+                w = HI[n // 6, n // 3 % 2, n % 3, a].reshape(768, 256)
                 acc = acc + nt(cot_pre[:, 256 * n : 256 * n + 256], w)
             cols = pl.ds(pl.multiple_of(a * 768, 256), 768)
             tmix[:, cols] = acc
@@ -704,13 +699,13 @@
         @pl.loop(0, 6, unroll=True)
         def _(t):
             cols = pl.ds(pl.multiple_of(cc * 1536 + t * 256, 256), 256)
-            w = HI[cc, t].reshape(D, 256)
+            w = HI[cc, t // 3, t % 3].reshape(D, 256)
             AA[256:512, cols] = (slope[:, cols] * nn(NT[256:512, :], w)).astype(BF16)
 
     @pl.loop(0, 6, unroll=True)
     def _(t):
         cols = pl.ds(pl.multiple_of(t * 256, 256), 256)
-        w = HO[t].reshape(FF, 256)
+        w = HO[t // 3, t % 3].reshape(FF, 256)
         tlater[:, cols] = (tmix[:, cols] + nn(AA[256:512, :], w)).astype(BF16)
 
     finish_sweep(1)
@@ -735,8 +730,8 @@
     vmem = pl.BlockSpec(memory_space=pltpu.VMEM)
     shapes = [
         ((2, 3, 2, 4, 4, 64, 128), BF16),
-        ((2, 6, 2, 4, 4, 48, 256), BF16),
-        ((6, 2, 4, 4, 2, 48, 256), BF16),
+        ((2, 2, 3, 2, 4, 4, 48, 256), BF16),
+        ((2, 3, 2, 4, 4, 2, 48, 256), BF16),
         ((24, 768), F32),
         ((24, 384), F32),
         ((48, 128), F32),

time: 139 us -> 132 us (0.950)
  Pallas kernels: 137 us -> 130 us
    pallas_call x1, Pallas kernels: 137 us -> 130 us  [body(): pl.pallas_call(kernel, out_shape=jax.ShapeDtypeStruct((48, ACT), F32), in...]
where the time goes in v5:
time: 132 us
  Pallas kernels  130 us (98%)
  local copies, waits for them, and re-layouts  1.38 us (1%)
    pallas_call x1, Pallas kernels, body(): pl.pallas_call(kernel, out_shape=jax.ShapeDtypeStruct((48, ACT), F32), in...  130 us

profile of v5, /device:TPU:0, one launch (start us, length us, event | category | flops | bytes accessed | tf_op | source)
XLA Modules:
  0.0 132.2 jit_solution(15166243906395508241)
XLA Ops:
  0.6 130.2 %natural_step.1 = f32[48,256]{1,0:T(8,128)} custom-call(bf16[256,1536]{1,0:T(8,128)(2,1)} %states.1, bf16[24,256]{1,0:T(8,128)(2,1)} %policy_in.1, bf16[4,1536]{1,0:T(4,128)(2,1)} %embed_in.1, bf16[1,24]{1,0:T(2,128)(2,1)} %bitcast.3, bf16[24,3072]{1,0:T(8,128)(2,1)} %inner_in.1, bf16[48,1536]{1,0:T(8,128)(2,1)} %outer_in.1, f32[1,256]{1,0:T(1,128)} %bitcast.2, ...), custom_call_target="tpu_custom_call" | custom-call | tf_op jit(solution)/shard_map/natural_step/pallas_call | solution.py:781
  130.9 1.4 %fusion = (f32[24,256]{1,0:T(8,128)}, f32[24,256]{1,0:T(8,128)}) fusion(f32[48,256]{1,0:T(8,128)} %natural_step.1), kind=kLoop, calls=%fused_computation | loop fusion | bytes 98304 | tf_op jit(solution)/shard_map/slice | solution.py:802

commit v6 on v5

--- a/solution.py
+++ b/solution.py
@@ -181,6 +181,8 @@
         cols = ALL if side is None else pl.ds(pl.multiple_of(side * 128, 128), 128)
         if item == 1:
             return HI.at[core, :, t, h, zz, yy, :, cols]
+        if item >= 5:
+            return HI.at[core, item - 5, t, h, zz, yy, :, cols]
         return HO.at[ALL if item == 2 else item - 3, t, h, zz, yy, core, :, cols]
 
     one = lambda i: pl.ds(i, 1)
@@ -271,13 +273,12 @@
     def item_whole(k, core):
         if k == 0:
             return S.at[core]
-        if k == 1:
-            return HI.at[core]
+        if k >= 5:
+            return HI.at[core, k - 5]
         return HO.at[k - 3, :, :, :, :, core]
 
     def hand(k, t, d):
-        if k == 1 or k == LAST:
-            ship(k, t, piece(t, 3, d), send_of[k], recv_of[k], partner)
+        ship(k, t, piece(t, 3, d), send_of[k], recv_of[(k, t, "hand")], partner)
 
     def stage_b(k):
         for t in range(3):
@@ -288,15 +289,17 @@
         for t in range(3):
             ring_pass(k, t, 2)
 
+    before = {0: 0, 5: 1, 3: 2}
+
     def stage_c(k):
         for t in range(3):
-            if k < LAST:
-                first_two_phases = min(k, 2)
-                arrived(first_two_phases, t, piece(t, 2, 2), (first_two_phases, t, 2, "far"))
+            if k in before:
+                arrived(before[k], t, piece(t, 2, 2), (before[k], t, 2, "far"))
             ring_start(k, t, 3)
         send_of[k] = sending(item_whole(k, c))
-        recv_of[k] = fresh(1)
+        shared = None if k == LAST else fresh(1)
         for t in range(3):
+            recv_of[(k, t, "hand")] = fresh(1) if k == LAST else shared
             hand(k, t, 0)
 
     def stage_pass(k):
@@ -314,13 +317,9 @@
         for t in range(3):
             arrived(k, t, piece(t, 3, 2), (k, t, 3, "far"))
             hand(k, t, 2)
-        if k == 0:
-            copy(S.at[c], S.at[c], send_of[k], recv_of[k], partner)
-        if k == 3:
-            copy(item_whole(k, c), item_whole(k, c), send_of[k], recv_of[k], partner)
 
     def stage_f(k):
-        take(recv_of[k], item_whole(k, 1 - c))
+        take(recv_of[(k, 0, "hand")], item_whole(k, 1 - c))
 
     scalar_sems = {}
     places = (("core", c, 2), ("y", y, 4), ("z", z, 4), ("x", x, 4))
@@ -408,17 +407,18 @@
     stage_g(0)
     stage_g(1)
     stage_c(0)
-    stage_c(1)
     total_step(0, 0)
+    stage_c(5)
+    total_step(0, 1)
     stage_pass(0)
-    total_step(0, 1)
+    stage_d(0)
 
     @pl.loop(0, 6)
     def _(i):
         s = pl.ds(pl.multiple_of(i * 256, 256), 256)
         start_t[s, :] = states[:, s].astype(F32).T.astype(BF16)
 
-    stage_c(3)
+    stage_c(6)
     stage_e(0)
     total_step(0, 2)
     stage_f(0)
@@ -451,9 +451,9 @@
     def blocks(n):
         return pl.loop(0, ROWS // n)
 
-    stage_pass(1)
-    stage_d(1)
-    stage_c(4)
+    stage_pass(5)
+    stage_d(5)
+    stage_c(3)
 
     first = jnp.tanh(nn(states[...], policy[...]))
     first_d[...] = 1.0 - first * first
@@ -484,9 +484,11 @@
 
     tangent_norm(256)
 
-    stage_e(1)
-    stage_pass(3)
-    stage_f(1)
+    stage_e(5)
+    stage_pass(6)
+    stage_d(6)
+    stage_c(4)
+    stage_f(5)
 
     def take_inner(ch, cc):
         @pl.loop(0, 3, unroll=True)
@@ -502,27 +504,33 @@
 
     take_inner(0, 0)
     take_inner(0, 1)
+    stage_e(6)
+    stage_pass(3)
+    stage_d(3)
+    stage_f(6)
+    take_inner(1, 0)
     stage_e(3)
-    take_inner(1, 0)
     stage_pass(4)
     take_inner(1, 1)
     stage_d(4)
     stage_f(3)
 
-    def take_outer(ch):
-        @pl.loop(0, 3, unroll=True)
-        def _(t):
-            w = HO[ch, t].reshape(FF, 256)
-            cols = pl.ds(pl.multiple_of(ch * 768 + t * 256, 256), 256)
-            l = (mixed[:, cols] + nn(AA[0:256, :], w)).astype(BF16)
-            later[:, cols] = l
-            later_t[cols, :] = l.astype(F32).T.astype(BF16)
-            tlater[:, cols] = (tmix[:, cols] + nn(AA[256:512, :], w)).astype(BF16)
-
-    take_outer(0)
+    def take_outer(ch, t):
+        w = HO[ch, t].reshape(FF, 256)
+        cols = pl.ds(pl.multiple_of(ch * 768 + t * 256, 256), 256)
+        l = (mixed[:, cols] + nn(AA[0:256, :], w)).astype(BF16)
+        later[:, cols] = l
+        later_t[cols, :] = l.astype(F32).T.astype(BF16)
+        tlater[:, cols] = (tmix[:, cols] + nn(AA[256:512, :], w)).astype(BF16)
+
+    @pl.loop(0, 3, unroll=True)
+    def _(t):
+        take_outer(0, t)
+
     stage_e(4)
-    stage_f(4)
-    take_outer(1)
+    for t in range(3):
+        take(recv_of[(LAST, t, "hand")], part(LAST, t, (ALL, ALL, ALL, None), 1 - c))
+        take_outer(1, t)
     take(g_sem, g32.at[1 - hi])
 
     second = jnp.tanh(nn(later[...], policy[...]))

time: 132 us -> 128 us (0.970)
  Pallas kernels: 130 us -> 126 us
    pallas_call x1, Pallas kernels: 130 us -> 126 us  [body(): pl.pallas_call(kernel, out_shape=jax.ShapeDtypeStruct((48, ACT), F32), in...]
where the time goes in v6:
time: 128 us
  Pallas kernels  126 us (98%)
  local copies, waits for them, and re-layouts  1.38 us (1%)
    pallas_call x1, Pallas kernels, body(): pl.pallas_call(kernel, out_shape=jax.ShapeDtypeStruct((48, ACT), F32), in...  126 us

profile of v6, /device:TPU:0, one launch (start us, length us, event | category | flops | bytes accessed | tf_op | source)
XLA Modules:
  0.0 128.2 jit_solution(4751140284636211637)
XLA Ops:
  0.6 126.2 %natural_step.1 = f32[48,256]{1,0:T(8,128)} custom-call(bf16[256,1536]{1,0:T(8,128)(2,1)} %states.1, bf16[24,256]{1,0:T(8,128)(2,1)} %policy_in.1, bf16[4,1536]{1,0:T(4,128)(2,1)} %embed_in.1, bf16[1,24]{1,0:T(2,128)(2,1)} %bitcast.3, bf16[24,3072]{1,0:T(8,128)(2,1)} %inner_in.1, bf16[48,1536]{1,0:T(8,128)(2,1)} %outer_in.1, f32[1,256]{1,0:T(1,128)} %bitcast.2, ...), custom_call_target="tpu_custom_call" | custom-call | tf_op jit(solution)/shard_map/natural_step/pallas_call | solution.py:789
  126.8 1.4 %fusion = (f32[24,256]{1,0:T(8,128)}, f32[24,256]{1,0:T(8,128)}) fusion(f32[48,256]{1,0:T(8,128)} %natural_step.1), kind=kLoop, calls=%fused_computation | loop fusion | bytes 98304 | tf_op jit(solution)/shard_map/slice | solution.py:810

commit v7 on v6

--- a/solution.py
+++ b/solution.py
@@ -20,8 +20,8 @@
 ACT = 256
 TOTAL_ROWS = 32768
 LAST = 4
-N_SEND = 90
-N_RECV = 124
+N_SEND = 75
+N_RECV = 108
 
 
 def nn(left, right):
@@ -629,17 +629,20 @@
             axis, own = ("z", z) if a == 0 else ("y", y)
             for d in (2, 1, 3):
                 copy(T2W.at[it, a, (own + d) % 4], R2.at[it, a, d - 1], s_sem, second_sems[a], axis_dev(axis, d))
+        third_sems = []
         for a in range(2):
             take(second_sems[a], R2.at[it, a])
             v = T2[it, a, z if a == 0 else y]
             for d in range(3):
                 v = v + R2[it, a, d].astype(F32)
             T3[it, x, a] = v.astype(BF16)
-        three = T3.at[it, pl.ds(0, 3)]
-        s_sem, r_sem = sending(three), fresh(1)
-        for d in (2, 1, 3):
-            copy(T3.at[it, x], T3.at[it, x], s_sem, r_sem, axis_dev("x", d))
-        take(r_sem, three)
+            three = T3.at[it, pl.ds(0, 3), a]
+            s_sem = sending(three)
+            third_sems.append(fresh(1))
+            for d in (2, 1, 3):
+                copy(T3.at[it, x, a], T3.at[it, x, a], s_sem, third_sems[a], axis_dev("x", d))
+        for a in range(2):
+            take(third_sems[a], T3.at[it, pl.ds(0, 3), a])
         return total
 
     def summed(it, h):

time: 128 us -> 128 us (level)
  no operation moved by 1% of the time
where the time goes in v7:
time: 128 us
  Pallas kernels  126 us (98%)
  local copies, waits for them, and re-layouts  1.38 us (1%)
    pallas_call x1, Pallas kernels, body(): pl.pallas_call(kernel, out_shape=jax.ShapeDtypeStruct((48, ACT), F32), in...  126 us

profile of v7, /device:TPU:0, one launch (start us, length us, event | category | flops | bytes accessed | tf_op | source)
XLA Modules:
  0.0 127.6 jit_solution(5499643869180205241)
XLA Ops:
  0.6 125.6 %natural_step.1 = f32[48,256]{1,0:T(8,128)} custom-call(bf16[256,1536]{1,0:T(8,128)(2,1)} %states.1, bf16[24,256]{1,0:T(8,128)(2,1)} %policy_in.1, bf16[4,1536]{1,0:T(4,128)(2,1)} %embed_in.1, bf16[1,24]{1,0:T(2,128)(2,1)} %bitcast.3, bf16[24,3072]{1,0:T(8,128)(2,1)} %inner_in.1, bf16[48,1536]{1,0:T(8,128)(2,1)} %outer_in.1, f32[1,256]{1,0:T(1,128)} %bitcast.2, ...), custom_call_target="tpu_custom_call" | custom-call | tf_op jit(solution)/shard_map/natural_step/pallas_call | solution.py:792
  126.2 1.4 %fusion = (f32[24,256]{1,0:T(8,128)}, f32[24,256]{1,0:T(8,128)}) fusion(f32[48,256]{1,0:T(8,128)} %natural_step.1), kind=kLoop, calls=%fused_computation | loop fusion | bytes 98304 | tf_op jit(solution)/shard_map/slice | solution.py:813
